TPU v7x, 256 devices: a whole 4x4x8 slice. The times are simulated.
256 devices in a mesh: row: 32 (over z_hi, x, core), col: 8 (over z_lo, y).
Axes of the slice: x: 4, y: 4, z: 8 (z_hi: 4, z_lo: 2; z = z_hi * 2 + z_lo), core: 2. Of those that a mesh axis runs over, the one named last changes fastest.
Arguments:
- mask: float32 [4096, 1024], P('row', 'col'), may hold values from 0 to 1
- mask_prev: float32 [4096, 1024], P('row', 'col'), may hold values from 0 to 1
- target: float32 [4096, 1024], P('row', 'col'), may hold values from 0 to 1
- kernels: float32 [8, 2, 129, 129], replicated, may hold values from -0.01953125 to 0.01953125
- restart: int32 [2, 32, 8], P(None, 'row', 'col'), may hold values from 0 to 1
Outputs:
- mask_next: float32 [4096, 1024], P('row', 'col')
- mask_last: float32 [4096, 1024], P('row', 'col')
- objective: float32 [2], replicated
All inputs are finite; a program needn't handle non-finite values.
Results may differ from a plain program's by a relative error of at most 0.0001.
Values sent between devices are 32-bit elements; how exact they have to be, the bound alone decides.
A program may use at most 128 MiB of HBM per device.

v0:
```python
import math

import jax
import jax.numpy as jnp
from jax import lax
from jax.sharding import PartitionSpec as P

ITERS = 2


SLOPE = 4.0
LEVEL = 0.8
STEP_SIZE = 0.05
TV_WEIGHT = 0.05
L1_WEIGHT = 0.5
EPS_TV = 0.01
PRIOR_STEPS = 10.0


def with_halo(x, sides, width):
    for axis, dim in sides:
        peers, length = (lax.axis_size(axis), x.shape[dim])
        up = [(i, (i + 1) % peers) for i in range(peers - 1)]
        down = [(j, i) for i, j in up]
        last = lax.slice_in_dim(x, length - width, length, axis=dim)
        initial = lax.slice_in_dim(x, 0, width, axis=dim)
        before = lax.ppermute(last, axis, up)
        after = lax.ppermute(initial, axis, down)
        x = jnp.concatenate([before, x, after], axis=dim)
    return x


def twiddle(offset, number, period, extent):
    frequency = jnp.arange(number, dtype=jnp.int32)[:, None] + offset
    position = jnp.arange(extent, dtype=jnp.int32)[None, :]
    phases = (frequency * position % period).astype(jnp.float32) * (2.0 * math.pi / period)
    return (jnp.cos(phases), jnp.sin(phases))


def multiply(left_arr, right_arr):
    return jnp.matmul(left_arr, right_arr, precision=lax.Precision.HIGHEST)


def apply_left(tables, direction_sign, real_part, imag_part):
    cos_part, sin_part = tables
    if imag_part is None:
        return (multiply(cos_part, real_part), direction_sign * multiply(sin_part, real_part))
    return (
        multiply(cos_part, real_part) - direction_sign * multiply(sin_part, imag_part),
        multiply(cos_part, imag_part) + direction_sign * multiply(sin_part, real_part),
    )


def apply_right(real_part, imag_part, tables, direction_sign):
    cos_part, sin_part = tables
    return (
        multiply(real_part, cos_part) - direction_sign * multiply(imag_part, sin_part),
        multiply(imag_part, cos_part) + direction_sign * multiply(real_part, sin_part),
    )


def kernel_spectrum(real_part, imag_part, len_rows, len_cols):
    support = real_part.shape[-1]
    spec_real, spec_imag = apply_left(
        twiddle(0, len_rows, len_rows, support), -1.0, real_part, imag_part
    )
    return apply_right(spec_real, spec_imag, twiddle(0, support, len_cols, len_cols), -1.0)


def forward_field(padded, spectrum, radius, out_rows, out_cols):
    len_rows, len_cols = padded.shape
    spec_real, spec_imag = apply_left(twiddle(0, len_rows, len_rows, len_rows), -1.0, padded, None)
    spec_real, spec_imag = apply_right(
        spec_real, spec_imag, twiddle(0, len_cols, len_cols, len_cols), -1.0
    )
    kernel_real, kernel_imag = spectrum
    prod_real = spec_real * kernel_real - spec_imag * kernel_imag
    prod_imag = spec_real * kernel_imag + spec_imag * kernel_real
    back_real, back_imag = apply_left(
        twiddle(2 * radius, out_rows, len_rows, len_rows), 1.0, prod_real, prod_imag
    )
    cos_part, sin_part = twiddle(2 * radius, out_cols, len_cols, len_cols)
    back_real, back_imag = apply_right(back_real, back_imag, (cos_part.T, sin_part.T), 1.0)
    scale = 1.0 / (len_rows * len_cols)
    return (back_real * scale, back_imag * scale)


def adjoint_field(source_real, source_imag, spectrum, radius, out_rows, out_cols):
    len_rows, len_cols = (source_real.shape[1], source_real.shape[2])
    spec_real, spec_imag = apply_left(
        twiddle(0, len_rows, len_rows, len_rows), -1.0, source_real, source_imag
    )
    spec_real, spec_imag = apply_right(
        spec_real, spec_imag, twiddle(0, len_cols, len_cols, len_cols), -1.0
    )
    kernel_real, kernel_imag = spectrum
    summed_real = jnp.sum(spec_real * kernel_real - spec_imag * kernel_imag, axis=0)
    summed_imag = jnp.sum(spec_real * kernel_imag + spec_imag * kernel_real, axis=0)
    back_real, back_imag = apply_left(
        twiddle(2 * radius, out_rows, len_rows, len_rows), 1.0, summed_real, summed_imag
    )
    cos_part, sin_part = twiddle(2 * radius, out_cols, len_cols, len_cols)
    return (multiply(back_real, cos_part.T) - multiply(back_imag, sin_part.T)) / (
        len_rows * len_cols
    )


def shards(mask, mask_prev, target, kernels, restart):
    tile_rows, tile_cols = mask.shape
    number = kernels.shape[0]
    support = kernels.shape[2]
    radius = (support - 1) // 2
    grid_rows = tile_rows * lax.axis_size("row")
    grid_cols = tile_cols * lax.axis_size("col")
    first_row = lax.axis_index("row") * tile_rows
    first_col = lax.axis_index("col") * tile_cols
    kernel_real = kernels[:, 0]
    kernel_imag = kernels[:, 1]
    near_rows = tile_rows + 2 * radius
    near_cols = tile_cols + 2 * radius
    adjoint_spectrum = kernel_spectrum(kernel_real, -kernel_imag, near_rows, near_cols)
    flipped_real = kernel_real[:, ::-1, ::-1]
    flipped_imag = kernel_imag[:, ::-1, ::-1]
    forward_spectrum = kernel_spectrum(flipped_real, flipped_imag, near_rows, near_cols)
    row_first = (jnp.arange(tile_rows) + first_row >= 1).astype(jnp.float32)[:, None]
    col_first = (jnp.arange(tile_cols) + first_col >= 1).astype(jnp.float32)[None, :]
    current = mask
    previous = mask_prev
    totals = []
    for iteration in range(ITERS):
        momentum = (iteration + PRIOR_STEPS - 1.0) / (iteration + PRIOR_STEPS + 2.0)
        keep_share = 1.0 - restart[iteration, 0, 0].astype(jnp.float32)
        extrapolated = current + keep_share * momentum * (current - previous)
        padded = with_halo(extrapolated, (("row", 0), ("col", 1)), radius)
        field_real, field_imag = forward_field(
            padded, forward_spectrum, radius, tile_rows, tile_cols
        )
        intensity = jnp.sum(field_real * field_real + field_imag * field_imag, axis=0)
        resist = jax.nn.sigmoid(SLOPE * (intensity - LEVEL))
        weight = 2.0 * (resist - target) * SLOPE * resist * (1.0 - resist)
        stacked = jnp.concatenate((weight * field_real, weight * field_imag), axis=0)
        spread = with_halo(stacked, (("row", 1), ("col", 2)), radius)
        source_real = spread[:number]
        source_imag = spread[number:]
        grad_data = 2.0 * adjoint_field(
            source_real, source_imag, adjoint_spectrum, radius, tile_rows, tile_cols
        )
        window_cells = padded[
            radius - 1 : radius + tile_rows + 1, radius - 1 : radius + tile_cols + 1
        ]
        center = window_cells[:-1, :-1]
        step_down = window_cells[1:, :-1] - center
        step_side = window_cells[:-1, 1:] - center
        length = jnp.sqrt(step_down * step_down + step_side * step_side + EPS_TV)
        flow_down = step_down / length
        flow_side = step_side / length
        grad_tv = (
            -(flow_down[1:, 1:] + flow_side[1:, 1:])
            + flow_down[:-1, 1:] * row_first
            + flow_side[1:, :-1] * col_first
        )
        local_term = (
            jnp.sum((resist - target) ** 2)
            + TV_WEIGHT * jnp.sum(length[1:, 1:])
            + L1_WEIGHT * jnp.sum(jnp.abs(extrapolated))
        )
        totals.append(lax.psum(local_term, ("row", "col")) / (grid_rows * grid_cols))
        updated = jnp.clip(
            extrapolated - STEP_SIZE * (grad_data + TV_WEIGHT * grad_tv) - STEP_SIZE * L1_WEIGHT,
            0.0,
            1.0,
        )
        previous = current
        current = updated
    objective = jnp.stack(totals)
    return (current, previous, objective)


def solution(mesh):
    in_specs = (P("row", "col"), P("row", "col"), P("row", "col"), P(), P(None, "row", "col"))
    out_specs = (P("row", "col"), P("row", "col"), P())
    return jax.shard_map(shards, mesh=mesh, in_specs=in_specs, out_specs=out_specs, check_vma=False)
```

profile of v0, /device:TPU:1, one launch (start us, length us, event | category | flops | bytes accessed | tf_op | source)
XLA Modules:
  0.0 429.2 jit_solution(14539724839730318175)
XLA Ops:
  4.2 4.5 %collective-permute-start = (f32[64,128]{1,0:T(8,128)S(1)}, f32[64,128]{1,0:T(8,128)S(1)}, u32[]{:S(2)}, u32[]{:S(2)}) collective-permute-start(f32[64,128]{1,0:T(8,128)S(1)} %get-tuple-element.40), channel_id=1, source_target_pairs={{0,8},{8,16},{16,24},{24,32},{32,40},{40,48},{48,56},{56,64},{64,7... | collective-permute-start | bytes 98312 | tf_op jit(solution)/shard_map/ppermute | solution.py:27
  10.6 5.0 %fusion.570 = (f32[8,1,129,129]{3,1,2,0:T(1,128)}, f32[8,1,129,129]{3,1,2,0:T(1,128)S(1)}) fusion(f32[8,2,129,129]{3,1,2,0:T(2,128)} %param.8), kind=kLoop, calls=%fused_computation.592 | loop fusion | bytes 2130048 | tf_op jit(solution)/shard_map/slice | solution.py:118
  16.5 2.6 fusion.132
  19.1 3.4 reverse
  22.5 2.6 fusion.136
  25.1 2.5 copy.21
  27.5 2.6 fusion.76
  30.1 11.8 %reverse.1 = f32[8,256,136]{1,2,0:T(8,128)} reverse(f32[8,256,136]{1,2,0:T(8,128)S(1)} %bitcast.217), dimensions={1,2} | reverse | bytes 2228224
  41.9 3.0 fusion.134
  46.7 3.9 fusion.125
  52.3 4.1 fusion.123
  56.4 3.9 multiply_subtract_fusion.7
  60.4 5.3 %multiply_add_fusion.7 = f32[8,256,256]{2,1,0:T(8,128)} fusion(f32[8,256,256]{2,1,0:T(8,128)S(1)} %fusion.123, f32[8,256,129]{1,2,0:T(8,128)S(1)} %fusion.55), kind=kOutput, calls=%fused_computation.38 | convolution fusion | flops 813108736 | bytes 5251072 | tf_op jit(solution)/shard_map/dot_general | solution.py:41
  68.8 5.7 %fusion.119 = f32[8,256,256]{2,1,0:T(8,128)} fusion(f32[8,256,129]{1,2,0:T(8,128)S(1)} %fusion.49), kind=kOutput, calls=%fused_computation.187 | convolution fusion | flops 812060160 | bytes 3153920 | tf_op jit(solution)/shard_map/dot_general | solution.py:41
  76.6 4.0 collective-permute-start.2
  94.3 2.3 fusion.81
  100.3 2.1 fusion.59
  107.4 3.8 collective-permute-start.4
  111.2 2.3 collective-permute-start.5
  113.5 5.3 %fusion.121 = f32[8,256,256]{2,1,0:T(8,128)} fusion(f32[8,256,129]{1,2,0:T(8,128)S(1)} %fusion.51), kind=kOutput, calls=%fused_computation.189 | convolution fusion | flops 812060160 | bytes 3153920 | tf_op jit(solution)/shard_map/dot_general | solution.py:41
  118.8 5.3 %multiply_add_fusion.3 = f32[8,256,256]{2,1,0:T(8,128)} fusion(f32[8,256,256]{2,1,0:T(8,128)S(1)} %copy-done.10, f32[8,256,129]{1,2,0:T(8,128)S(1)} %fusion.51), kind=kOutput, calls=%fused_computation.30 | convolution fusion | flops 813108736 | bytes 5251072 | tf_op jit(solution)/shard_map/dot_general | solution.py:41
  125.8 2.8 fusion.572
  128.6 3.2 copy.12
  131.8 5.2 %collective-permute-start.6 = (f32[16,256,64]{1,2,0:T(8,128)}, f32[16,256,64]{1,2,0:T(8,128)}, u32[]{:S(2)}, u32[]{:S(2)}) collective-permute-start(f32[16,256,64]{1,2,0:T(8,128)} %copy.12), channel_id=1, source_target_pairs={{0,1},{1,2},{2,3},{3,4},{4,5},{5,6},{6,7},{8,9},{9,10},{10,11},{11... | collective-permute-start | bytes 3145736 | tf_op jit(solution)/shard_map/ppermute | solution.py:27
  137.0 3.2 copy.13
  142.0 6.9 %multiply_subtract_fusion.3 = f32[8,256,256]{2,1,0:T(8,128)} fusion(f32[8,256,256]{2,1,0:T(8,128)} %fusion.121, f32[8,256,129]{1,2,0:T(8,128)S(1)} %copy-done.9), kind=kOutput, calls=%fused_computation.32 | convolution fusion | flops 813108736 | bytes 5251072 | tf_op jit(solution)/shard_map/dot_general | solution.py:41
  150.6 7.4 %collective-permute-done.6 = f32[16,256,64]{1,2,0:T(8,128)} collective-permute-done((f32[16,256,64]{1,2,0:T(8,128)}, f32[16,256,64]{1,2,0:T(8,128)}, u32[]{:S(2)}, u32[]{:S(2)}) %collective-permute-start.6) | collective-permute-done | bytes 1048608 | tf_op jit(solution)/shard_map/ppermute | solution.py:27
  158.0 3.2 copy.14
  161.3 5.0 %collective-permute-done.7 = f32[16,256,64]{1,2,0:T(8,128)} collective-permute-done((f32[16,256,64]{1,2,0:T(8,128)}, f32[16,256,64]{1,2,0:T(8,128)}, u32[]{:S(2)}, u32[]{:S(2)}) %collective-permute-start.7) | collective-permute-done | bytes 1048608 | tf_op jit(solution)/shard_map/ppermute | solution.py:28
  166.3 3.2 copy.15
  169.5 5.4 %pad_maximum_fusion = f32[16,256,256]{2,1,0:T(8,128)S(1)} fusion(f32[16,256,64]{2,1,0:T(8,128)} %copy.15, f32[16,64,128]{2,1,0:T(8,128)} %copy-done.21, f32[8,128,128]{2,1,0:T(8,128)S(1)} %copy-done.15, f32[8,128,128]{2,1,0:T(8,128)S(1)} %copy-done.13, f32[16,64,128]{2,1,0:T(8,128)} %copy-done.20, f32[16,256,64]{2,1,0:T(8,128)} %copy.14), kind=kLoop, calls=%fused_computation | loop fusion | flops 5242880 | bytes 8388608 | tf_op jit(solution)/shard_map/concatenate | solution.py:29
  175.0 2.9 fusion.26
  177.9 2.9 fusion.28
  180.8 3.1 multiply_add_fusion.5
  183.8 2.8 fusion.10
  186.7 3.2 fusion.8
  189.9 3.1 multiply_subtract_fusion.5
  193.0 2.8 multiply_subtract_fusion.4
  195.9 3.5 add_reduce_fusion.1
  203.8 3.2 abs_reduce_fusion
  207.0 4.6 %collective-permute-start.8 = (f32[64,128]{1,0:T(8,128)S(1)}, f32[64,128]{1,0:T(8,128)S(1)}, u32[]{:S(2)}, u32[]{:S(2)}) collective-permute-start(f32[64,128]{1,0:T(8,128)S(1)} %get-tuple-element.36), channel_id=1, source_target_pairs={{0,8},{8,16},{16,24},{24,32},{32,40},{40,48},{48,56},{56,64},{64,7... | collective-permute-start | bytes 98312 | tf_op jit(solution)/shard_map/ppermute | solution.py:27
  213.6 3.3 collective-permute-done.9
  217.0 3.0 collective-permute-start.10
  221.9 6.6 %collective-permute-done.11 = f32[256,64]{1,0:T(8,128)S(1)} collective-permute-done((f32[256,64]{1,0:T(8,128)S(1)}, f32[256,64]{1,0:T(8,128)S(1)}, u32[]{:S(2)}, u32[]{:S(2)}) %collective-permute-start.11) | collective-permute-done | bytes 65568 | tf_op jit(solution)/shard_map/ppermute | solution.py:28
  239.1 2.6 fusion.83
  245.3 2.2 fusion.57
  253.0 3.1 collective-permute-start.12
  258.0 4.2 collective-permute-done.12
  262.2 4.4 %collective-permute-done.13 = f32[16,64,128]{2,1,0:T(8,128)S(1)} collective-permute-done((f32[16,64,128]{2,1,0:T(8,128)S(1)}, f32[16,64,128]{2,1,0:T(8,128)S(1)}, u32[]{:S(2)}, u32[]{:S(2)}) %collective-permute-start.13) | collective-permute-done | bytes 524320 | tf_op jit(solution)/shard_map/ppermute | solution.py:28
  267.5 2.8 fusion.571
  270.3 3.3 copy.16
  273.6 6.7 %collective-permute-start.14 = (f32[16,256,64]{1,2,0:T(8,128)}, f32[16,256,64]{1,2,0:T(8,128)}, u32[]{:S(2)}, u32[]{:S(2)}) collective-permute-start(f32[16,256,64]{1,2,0:T(8,128)} %copy.16), channel_id=1, source_target_pairs={{0,1},{1,2},{2,3},{3,4},{4,5},{5,6},{6,7},{8,9},{9,10},{10,11},{11... | collective-permute-start | bytes 3145736 | tf_op jit(solution)/shard_map/ppermute | solution.py:27
  289.7 95.7 %all-reduce = (f32[]{:T(128)}, f32[]{:T(128)}) all-reduce(f32[]{:T(128)S(6)} %add.489, f32[]{:T(128)S(6)} %add.487), channel_id=1, replica_groups=mesh['row'=32,'col'=8] {'row','col'}, use_global_device_ids=true, to_apply=%region_13.14 | all-reduce | flops 2 | bytes 16 | tf_op jit(solution)/shard_map/psum | solution.py:167
  389.9 3.2 copy.19
  393.1 5.0 %pad_maximum_fusion.1 = f32[16,256,256]{2,1,0:T(8,128)S(1)} fusion(f32[16,256,64]{2,1,0:T(8,128)} %copy.19, f32[16,64,128]{2,1,0:T(8,128)} %copy-done.19, f32[8,128,128]{2,1,0:T(8,128)S(1)} %get-tuple-element.35, f32[8,128,128]{2,1,0:T(8,128)S(1)} %get-tuple-element.34, f32[16,64,128]{2,1,0:T(8,128)} %copy-done.18, f32[16,256,64]{2,1,0:T(8,128)S(1)} %copy.18), kind=kLoop, calls=%fused_computation.1 | loop fusion | flops 5242880 | bytes 8388608 | tf_op jit(solution)/shard_map/concatenate | solution.py:29
  398.1 2.9 fusion.18
  401.0 2.9 fusion.20
  403.9 3.1 multiply_add_fusion.1
  407.0 2.8 fusion.2
  409.9 3.0 fusion
  412.8 3.0 multiply_subtract_fusion.1
  415.9 2.8 multiply_subtract_fusion
  418.7 3.3 add_reduce_fusion
  426.5 2.4 fusion.73
  (161 shorter events, 84.9 us)
Async XLA Ops:
  4.2 71.0 %collective-permute-start = (f32[64,128]{1,0:T(8,128)S(1)}, f32[64,128]{1,0:T(8,128)S(1)}, u32[]{:S(2)}, u32[]{:S(2)}) collective-permute-start(f32[64,128]{1,0:T(8,128)S(1)} %get-tuple-element.40), channel_id=1, source_target_pairs={{0,8},{8,16},{16,24},{24,32},{32,40},{40,48},{48,56},{56,64},{64,7... | collective-permute-start | bytes 98312 | tf_op jit(solution)/shard_map/ppermute | solution.py:27
  8.7 66.5 %collective-permute-start.1 = (f32[64,128]{1,0:T(8,128)S(1)}, f32[64,128]{1,0:T(8,128)S(1)}, u32[]{:S(2)}, u32[]{:S(2)}) collective-permute-start(f32[64,128]{1,0:T(8,128)S(1)} %get-tuple-element.41), channel_id=1, source_target_pairs={{8,0},{16,8},{24,16},{32,24},{40,32},{48,40},{56,48},{64,56},{72,6... | collective-permute-start | bytes 98312 | tf_op jit(solution)/shard_map/ppermute | solution.py:28
  22.4 2.6 copy-start.22
  27.5 14.4 %copy-start.6 = (f32[8,1,129,129]{2,3,0,1:T(8,128)}, f32[8,1,129,129]{2,3,0,1:T(8,128)S(1)}, u32[]{:S(2)}) copy-start(f32[8,1,129,129]{2,3,0,1:T(8,128)S(1)} %copy.21) | copy-start | bytes 1597540
  41.9 3.0 copy-start.24
  41.9 3.0 copy-start.37
  46.6 4.0 copy-start.23
  60.4 5.3 %copy-start.17 = (f32[256,8,129]{0,2,1:T(8,128)S(1)}, f32[256,8,129]{0,2,1:T(8,128)}, u32[]{:S(2)}) copy-start(f32[256,8,129]{0,2,1:T(8,128)} %fusion.76) | copy-start | bytes 3170308
  65.6 1.6 copy-start.7
  65.6 1.6 copy-start.16
  67.2 7.2 %copy-start.8 = (f32[8,256,129]{1,2,0:T(8,128)}, f32[8,256,129]{1,2,0:T(8,128)S(1)}, u32[]{:S(2)}) copy-start(f32[8,256,129]{1,2,0:T(8,128)S(1)} %fusion.49) | copy-start | bytes 3170308
  75.3 7.1 %collective-permute-start.3 = (f32[256,64]{1,0:T(8,128)S(1)}, f32[256,64]{1,0:T(8,128)S(1)}, u32[]{:S(2)}, u32[]{:S(2)}) collective-permute-start(f32[256,64]{1,0:T(8,128)S(1)} %get-tuple-element.33), channel_id=1, source_target_pairs={{1,0},{2,1},{3,2},{4,3},{5,4},{6,5},{7,6},{9,8},{10,9},{11,10},{12... | collective-permute-start | bytes 196616 | tf_op jit(solution)/shard_map/ppermute | solution.py:28
  76.6 7.2 %collective-permute-start.2 = (f32[256,64]{1,0:T(8,128)S(1)}, f32[256,64]{1,0:T(8,128)S(1)}, u32[]{:S(2)}, u32[]{:S(2)}) collective-permute-start(f32[256,64]{1,0:T(8,128)S(1)} %get-tuple-element.32), channel_id=1, source_target_pairs={{0,1},{1,2},{2,3},{3,4},{4,5},{5,6},{6,7},{8,9},{9,10},{10,11},{11... | collective-permute-start | bytes 196616 | tf_op jit(solution)/shard_map/ppermute | solution.py:27
  82.4 5.7 %copy-start.27 = (f32[256,64]{1,0:T(8,128)}, f32[256,64]{1,0:T(8,128)S(1)}, u32[]{:S(2)}) copy-start(f32[256,64]{1,0:T(8,128)S(1)} %collective-permute-done.3) | copy-start | bytes 196612
  83.8 4.3 copy-start.32
  88.0 4.1 copy-start
  104.0 3.1 copy-start.29
  107.3 16.8 %copy-start.12 = (f32[8,128,128]{2,1,0:T(8,128)}, f32[8,128,128]{2,1,0:T(8,128)S(1)}, u32[]{:S(2)}) copy-start(f32[8,128,128]{2,1,0:T(8,128)S(1)} %get-tuple-element.38) | copy-start | bytes 1572868
  107.3 16.8 %copy-start.14 = (f32[8,128,128]{2,1,0:T(8,128)}, f32[8,128,128]{2,1,0:T(8,128)S(1)}, u32[]{:S(2)}) copy-start(f32[8,128,128]{2,1,0:T(8,128)S(1)} %get-tuple-element.39) | copy-start | bytes 1572868
  107.4 11.4 %copy-start.10 = (f32[8,256,256]{2,1,0:T(8,128)S(1)}, f32[8,256,256]{2,1,0:T(8,128)}, u32[]{:S(2)}) copy-start(f32[8,256,256]{2,1,0:T(8,128)} %fusion.119) | copy-start | bytes 6291460
  107.4 16.7 %collective-permute-start.4 = (f32[16,64,128]{2,1,0:T(8,128)S(1)}, f32[16,64,128]{2,1,0:T(8,128)S(1)}, u32[]{:S(2)}, u32[]{:S(2)}) collective-permute-start(f32[16,64,128]{2,1,0:T(8,128)S(1)} %get-tuple-element.27), channel_id=1, source_target_pairs={{0,8},{8,16},{16,24},{24,32},{32,40},{40,48},{48,56},{56,64},{64,7... | collective-permute-start | bytes 1572872 | tf_op jit(solution)/shard_map/ppermute | solution.py:27
  111.2 12.9 %collective-permute-start.5 = (f32[16,64,128]{2,1,0:T(8,128)S(1)}, f32[16,64,128]{2,1,0:T(8,128)S(1)}, u32[]{:S(2)}, u32[]{:S(2)}) collective-permute-start(f32[16,64,128]{2,1,0:T(8,128)S(1)} %get-tuple-element.28), channel_id=1, source_target_pairs={{8,0},{16,8},{24,16},{32,24},{40,32},{48,40},{56,48},{64,56},{72,6... | collective-permute-start | bytes 1572872 | tf_op jit(solution)/shard_map/ppermute | solution.py:28
  124.1 0.8 copy-start.20
  124.9 0.8 copy-start.21
  131.8 10.2 %copy-start.9 = (f32[8,256,129]{1,2,0:T(8,128)S(1)}, f32[8,256,129]{1,2,0:T(8,128)}, u32[]{:S(2)}) copy-start(f32[8,256,129]{1,2,0:T(8,128)} %copy-done.8) | copy-start | bytes 3170308
  131.8 26.3 %collective-permute-start.6 = (f32[16,256,64]{1,2,0:T(8,128)}, f32[16,256,64]{1,2,0:T(8,128)}, u32[]{:S(2)}, u32[]{:S(2)}) collective-permute-start(f32[16,256,64]{1,2,0:T(8,128)} %copy.12), channel_id=1, source_target_pairs={{0,1},{1,2},{2,3},{3,4},{4,5},{5,6},{6,7},{8,9},{9,10},{10,11},{11... | collective-permute-start | bytes 3145736 | tf_op jit(solution)/shard_map/ppermute | solution.py:27
  140.2 26.1 %collective-permute-start.7 = (f32[16,256,64]{1,2,0:T(8,128)}, f32[16,256,64]{1,2,0:T(8,128)}, u32[]{:S(2)}, u32[]{:S(2)}) collective-permute-start(f32[16,256,64]{1,2,0:T(8,128)} %copy.13), channel_id=1, source_target_pairs={{1,0},{2,1},{3,2},{4,3},{5,4},{6,5},{7,6},{9,8},{10,9},{11,10},{12... | collective-permute-start | bytes 3145736 | tf_op jit(solution)/shard_map/ppermute | solution.py:28
  142.0 6.9 %copy-start.33 = (f32[256,64]{1,0:T(8,128)S(1)}, f32[256,64]{1,0:T(8,128)}, u32[]{:S(2)}) copy-start(f32[256,64]{1,0:T(8,128)} %copy-done.32) | copy-start | bytes 196612
  142.0 7.0 %copy-start.28 = (f32[256,64]{1,0:T(8,128)S(1)}, f32[256,64]{1,0:T(8,128)}, u32[]{:S(2)}) copy-start(f32[256,64]{1,0:T(8,128)} %copy-done.27) | copy-start | bytes 196612
  161.3 8.3 %copy-start.13 = (f32[8,128,128]{2,1,0:T(8,128)S(1)}, f32[8,128,128]{2,1,0:T(8,128)}, u32[]{:S(2)}) copy-start(f32[8,128,128]{2,1,0:T(8,128)} %copy-done.12) | copy-start | bytes 1572868
  161.3 8.3 %copy-start.15 = (f32[8,128,128]{2,1,0:T(8,128)S(1)}, f32[8,128,128]{2,1,0:T(8,128)}, u32[]{:S(2)}) copy-start(f32[8,128,128]{2,1,0:T(8,128)} %copy-done.14) | copy-start | bytes 1572868
  193.0 2.9 copy-start.2
  193.0 2.9 copy-start.4
  199.4 4.4 %copy-start.34 = (f32[128,128]{1,0:T(8,128)S(1)}, f32[128,128]{1,0:T(8,128)}, u32[]{:S(2)}) copy-start(f32[128,128]{1,0:T(8,128)} %param.5) | copy-start | bytes 196612
  199.4 4.4 %copy-start.35 = (f32[128]{0:T(128)S(1)}, f32[128]{0:T(128)}, u32[]{:S(2)}) copy-start(f32[128]{0:T(128)} %get-tuple-element.50) | copy-start | bytes 1540
  207.0 6.5 %collective-permute-start.8 = (f32[64,128]{1,0:T(8,128)S(1)}, f32[64,128]{1,0:T(8,128)S(1)}, u32[]{:S(2)}, u32[]{:S(2)}) collective-permute-start(f32[64,128]{1,0:T(8,128)S(1)} %get-tuple-element.36), channel_id=1, source_target_pairs={{0,8},{8,16},{16,24},{24,32},{32,40},{40,48},{48,56},{56,64},{64,7... | collective-permute-start | bytes 98312 | tf_op jit(solution)/shard_map/ppermute | solution.py:27
  211.6 5.2 %collective-permute-start.9 = (f32[64,128]{1,0:T(8,128)S(1)}, f32[64,128]{1,0:T(8,128)S(1)}, u32[]{:S(2)}, u32[]{:S(2)}) collective-permute-start(f32[64,128]{1,0:T(8,128)S(1)} %get-tuple-element.37), channel_id=1, source_target_pairs={{8,0},{16,8},{24,16},{32,24},{40,32},{48,40},{56,48},{64,56},{72,6... | collective-permute-start | bytes 98312 | tf_op jit(solution)/shard_map/ppermute | solution.py:28
  217.0 4.9 %collective-permute-start.10 = (f32[256,64]{1,0:T(8,128)S(1)}, f32[256,64]{1,0:T(8,128)S(1)}, u32[]{:S(2)}, u32[]{:S(2)}) collective-permute-start(f32[256,64]{1,0:T(8,128)S(1)} %get-tuple-element.30), channel_id=1, source_target_pairs={{0,1},{1,2},{2,3},{3,4},{4,5},{5,6},{6,7},{8,9},{9,10},{10,11},{11... | collective-permute-start | bytes 196616 | tf_op jit(solution)/shard_map/ppermute | solution.py:27
  220.0 8.5 %collective-permute-start.11 = (f32[256,64]{1,0:T(8,128)S(1)}, f32[256,64]{1,0:T(8,128)S(1)}, u32[]{:S(2)}, u32[]{:S(2)}) collective-permute-start(f32[256,64]{1,0:T(8,128)S(1)} %get-tuple-element.31), channel_id=1, source_target_pairs={{1,0},{2,1},{3,2},{4,3},{5,4},{6,5},{7,6},{9,8},{10,9},{11,10},{12... | collective-permute-start | bytes 196616 | tf_op jit(solution)/shard_map/ppermute | solution.py:28
  221.9 10.9 %copy-start.31 = (f32[256,64]{1,0:T(8,128)}, f32[256,64]{1,0:T(8,128)S(1)}, u32[]{:S(2)}) copy-start(f32[256,64]{1,0:T(8,128)S(1)} %collective-permute-done.10) | copy-start | bytes 196612
  228.5 4.3 copy-start.25
  232.8 4.1 copy-start.1
  249.0 3.1 copy-start.30
  253.0 9.2 %collective-permute-start.12 = (f32[16,64,128]{2,1,0:T(8,128)S(1)}, f32[16,64,128]{2,1,0:T(8,128)S(1)}, u32[]{:S(2)}, u32[]{:S(2)}) collective-permute-start(f32[16,64,128]{2,1,0:T(8,128)S(1)} %get-tuple-element.25), channel_id=1, source_target_pairs={{0,8},{8,16},{16,24},{24,32},{32,40},{40,48},{48,56},{56,64},{64,7... | collective-permute-start | bytes 1572872 | tf_op jit(solution)/shard_map/ppermute | solution.py:27
  256.1 10.5 %collective-permute-start.13 = (f32[16,64,128]{2,1,0:T(8,128)S(1)}, f32[16,64,128]{2,1,0:T(8,128)S(1)}, u32[]{:S(2)}, u32[]{:S(2)}) collective-permute-start(f32[16,64,128]{2,1,0:T(8,128)S(1)} %get-tuple-element.26), channel_id=1, source_target_pairs={{8,0},{16,8},{24,16},{32,24},{40,32},{48,40},{56,48},{64,56},{72,6... | collective-permute-start | bytes 1572872 | tf_op jit(solution)/shard_map/ppermute | solution.py:28
  262.2 4.4 %copy-start.18 = (f32[16,64,128]{2,1,0:T(8,128)}, f32[16,64,128]{2,1,0:T(8,128)S(1)}, u32[]{:S(2)}) copy-start(f32[16,64,128]{2,1,0:T(8,128)S(1)} %collective-permute-done.12) | copy-start | bytes 1572868
  266.6 0.8 copy-start.19
  270.3 10.0 %copy-start.11 = (f32[16,256,64]{2,1,0:T(8,128)S(1)}, f32[16,256,64]{2,1,0:T(8,128)}, u32[]{:S(2)}) copy-start(f32[16,256,64]{2,1,0:T(8,128)} %get-tuple-element.22) | copy-start | bytes 3145732
  273.6 13.2 %copy-start.26 = (f32[256,64]{1,0:T(8,128)S(1)}, f32[256,64]{1,0:T(8,128)}, u32[]{:S(2)}) copy-start(f32[256,64]{1,0:T(8,128)} %copy-done.25) | copy-start | bytes 196612
  273.6 114.5 %collective-permute-start.14 = (f32[16,256,64]{1,2,0:T(8,128)}, f32[16,256,64]{1,2,0:T(8,128)}, u32[]{:S(2)}, u32[]{:S(2)}) collective-permute-start(f32[16,256,64]{1,2,0:T(8,128)} %copy.16), channel_id=1, source_target_pairs={{0,1},{1,2},{2,3},{3,4},{4,5},{5,6},{6,7},{8,9},{9,10},{10,11},{11... | collective-permute-start | bytes 3145736 | tf_op jit(solution)/shard_map/ppermute | solution.py:27
  281.9 108.1 %collective-permute-start.15 = (f32[16,256,64]{1,2,0:T(8,128)}, f32[16,256,64]{1,2,0:T(8,128)}, u32[]{:S(2)}, u32[]{:S(2)}) collective-permute-start(f32[16,256,64]{1,2,0:T(8,128)} %copy.17), channel_id=1, source_target_pairs={{1,0},{2,1},{3,2},{4,3},{5,4},{6,5},{7,6},{9,8},{10,9},{11,10},{12... | collective-permute-start | bytes 3145736 | tf_op jit(solution)/shard_map/ppermute | solution.py:28
  415.8 2.9 copy-start.3
  415.8 2.9 copy-start.5
  422.0 4.5 %copy-start.36 = (f32[128]{0:T(128)S(1)}, f32[128]{0:T(128)}, u32[]{:S(2)}) copy-start(f32[128]{0:T(128)} %get-tuple-element.50) | copy-start | bytes 1540
where the time goes:
time: 436 us; the launch traced here: 429 us
  matrix products  167 us (38%)
  blocking collectives  95.7 us (22%)
  local copies, waits for them, and re-layouts  55.7 us (13%)
  starting transfers between devices  48.1 us (11%)
  waiting for transfers between devices  34.8 us (8%)
  other arithmetic  19.7 us (5%)
  between operations  8.5 us (2%)
    dot_general x72, matrix products, multiply(): return jnp.matmul(left_arr, right_arr, precision=lax.Precision.HIGHEST)  167 us
    psum x1, blocking collectives, shards(): lax.psum(local_term, ('row', 'col')) / (grid_rows * grid_cols)  95.7 us
    ppermute x8, starting transfers between devices, with_halo(): before = lax.ppermute(last, axis, up)  34.8 us
    ppermute x8, waiting for transfers between devices, with_halo(): after = lax.ppermute(initial, axis, down)  21.1 us
    unnamed x80, local copies, waits for them, and re-layouts  21 us
    ppermute x8, waiting for transfers between devices, with_halo(): before = lax.ppermute(last, axis, up)  13.7 us
    ppermute x8, starting transfers between devices, with_halo(): after = lax.ppermute(initial, axis, down)  13.2 us
    slice x8, local copies, waits for them, and re-layouts, with_halo(): last = lax.slice_in_dim(x, length - width, length, axis=dim)  12.2 us
  transfers between devices with their start and end apart: 16, of which 9 were waited for; matrix products, arithmetic and copies ran while one was open for 23% of the time, Pallas kernels for 0%

commit v1 on v0

v1 whole, which is shorter than its diff:
```python
import functools
import math

import jax
import jax.numpy as jnp
import ml_dtypes
import numpy as np
from jax import lax
from jax.experimental import pallas as pl
from jax.experimental.pallas import tpu as pltpu
from jax.sharding import PartitionSpec as P

ITERS = 2
SLOPE = 4.0
LEVEL = 0.8
STEP_SIZE = 0.05
TV_WEIGHT = 0.05
L1_WEIGHT = 0.5
EPS_TV = 0.01
PRIOR_STEPS = 10.0

T = 128
N = 256
KS = 129
KP = 144
K = 8
R = 64
MESH = pl.DeviceIdType.MESH
F32 = jnp.float32
BF16 = jnp.bfloat16


def tables():
    pos = np.arange(N)
    shift = np.where(pos < T + R, pos, pos - N).astype(np.float64)
    tap = np.arange(N) - R
    alive = (np.arange(N) < KS).astype(np.float64)
    freq2 = np.arange(T) + 0.5
    freq1 = np.arange(N)
    step = 2.0 * math.pi / N

    def right(offset):
        phase = offset[:, None] * freq2[None, :] * step
        return np.concatenate([np.cos(phase), -np.sin(phase)], axis=1)

    def left(offset):
        phase = freq1[:, None] * offset[None, :] * step
        return np.concatenate([np.cos(phase), np.sin(phase)], axis=0)

    w = right(shift)
    wk = right(tap) * alive[:, None]
    d = left(pos)
    dk = left(tap) * alive[None, :]
    wi = w.T * (2.0 / (N * N))

    def half(odd):
        rows = 2 * np.arange(T // 2) + odd
        phase = rows[:, None] * np.arange(T)[None, :] * step
        c, s = np.cos(phase), np.sin(phase)
        return np.concatenate([np.concatenate([c, -s], 1), np.concatenate([s, c], 1)], 0)

    even, odd = half(0), half(1)
    both = np.concatenate([even.T, odd.T], axis=1)
    place, parts, row = {}, [], 0
    for name, table in (("w", w), ("wk", wk), ("d", d), ("dk", dk), ("even", even), ("odd", odd), ("both", both), ("wi", wi)):
        high = table.astype(np.float32).astype(ml_dtypes.bfloat16)
        low = (table - high.astype(np.float64)).astype(np.float32).astype(ml_dtypes.bfloat16)
        for which, part in (("h", high), ("l", low)):
            place[name + which] = (row, row + part.shape[0])
            parts.append(part)
            row += part.shape[0]
    return place, np.concatenate(parts, axis=0)


PLACE, TABLE = tables()


def split(x):
    high = x.astype(BF16)
    return high, (x - high.astype(F32)).astype(BF16)


def mm(a, b):
    return jnp.dot(a, b, preferred_element_type=F32)


def rows(*parts):
    return jnp.concatenate(parts, axis=0)


def lanes(*parts):
    return jnp.concatenate(parts, axis=1)


def kernel(
    size_r,
    size_c,
    mask_ref,
    prev_ref,
    target_ref,
    restart_ref,
    taps_hbm,
    table_hbm,
    next_ref,
    last_ref,
    goal_ref,
    taps_ref,
    table_ref,
    padded_ref,
    hr_ref,
    hi_ref,
    field_ref,
    gr_ref,
    gi_ref,
    point_ref,
    own_ref,
    ud_ref,
    lr_ref,
    corner_ref,
    goal_part,
    slots_ref,
    sums_ref,
    local_sem,
    send_sem,
    recv_sem,
    red_send,
    red_recv,
):
    r = lax.axis_index("row")
    c = lax.axis_index("col")
    near = []
    for dr, dc in ((1, 0), (-1, 0), (0, 1), (0, -1), (1, 1), (1, -1), (-1, 1), (-1, -1)):
        near.append((lax.rem(r + dr + size_r, size_r), lax.rem(c + dc + size_c, size_c)))
    low = min(8, size_r)
    high = size_r // low
    r_high, r_low = r // low, lax.rem(r, low)
    groups = []
    groups.append((c, [(r, lax.rem(c + d, size_c)) for d in range(1, size_c)]))
    groups.append((r_low, [(r_high * low + lax.rem(r_low + d, low), c) for d in range(1, low)]))
    groups.append((r_high, [(lax.rem(r_high + d, high) * low + r_low, c) for d in range(1, high)]))

    def tab(name):
        first, end = PLACE[name]
        return table_ref[first:end, :]

    taps_copy = pltpu.make_async_copy(taps_hbm, taps_ref, local_sem.at[0])
    table_copy = pltpu.make_async_copy(table_hbm, table_ref, local_sem.at[1])
    table_copy.start()
    taps_copy.start()
    barrier = pltpu.get_barrier_semaphore()
    everyone = near + [peer for _, peers in groups for peer in peers]
    for peer in everyone:
        pl.semaphore_signal(barrier, inc=1, device_id=peer, device_id_type=MESH)

    def extrapolate(t, current, previous):
        momentum = (t + PRIOR_STEPS - 1.0) / (t + PRIOR_STEPS + 2.0)
        keep = 1.0 - restart_ref[t, 0, 0].astype(F32)
        point_ref[t] = current + keep * momentum * (current - previous)

    def exchange(slot, down, up, side, corner_down, corner_up):
        copies = []
        pieces = (
            (down[0], ud_ref.at[slot, down[1]]),
            (up[0], ud_ref.at[slot, up[1]]),
            (side, lr_ref.at[slot, 0]),
            (side, lr_ref.at[slot, 1]),
            (corner_down, corner_ref.at[slot, 0, down[1]]),
            (corner_down, corner_ref.at[slot, 1, down[1]]),
            (corner_up, corner_ref.at[slot, 0, up[1]]),
            (corner_up, corner_ref.at[slot, 1, up[1]]),
        )
        for n, (source, target) in enumerate(pieces):
            copy = pltpu.make_async_remote_copy(
                src_ref=source,
                dst_ref=target,
                send_sem=send_sem.at[slot, n],
                recv_sem=recv_sem.at[slot, n],
                device_id=near[n],
                device_id_type=MESH,
            )
            copy.start()
            copies.append(copy)
        return copies

    top, bottom = pl.ds(0, R), pl.ds(R, R)

    def send_point(t):
        ref = point_ref.at[t]
        return exchange(2 * t, (ref.at[bottom], bottom), (ref.at[top], top), ref, ref.at[bottom], ref.at[top])

    def send_gradient(t):
        down, up = pl.ds(T, R), pl.ds(T + R, R)
        left_lanes, right_lanes = pl.ds(0, T), pl.ds(T, T)
        ref = own_ref.at[t]
        return exchange(
            2 * t + 1,
            (ref.at[down, left_lanes], top),
            (ref.at[up, left_lanes], bottom),
            ref.at[pl.ds(0, T), right_lanes],
            ref.at[down, right_lanes],
            ref.at[up, right_lanes],
        )

    def reduce_start(phase, value):
        me, peers = groups[phase]
        slots_ref[phase, me] = value
        sums_ref[phase] = value
        copies = []
        for d, peer in enumerate(peers):
            copy = pltpu.make_async_remote_copy(
                src_ref=sums_ref.at[phase],
                dst_ref=slots_ref.at[phase, me],
                send_sem=red_send.at[phase, d],
                recv_sem=red_recv.at[phase, d],
                device_id=peer,
                device_id_type=MESH,
            )
            copy.start()
            copies.append(copy)
        return copies

    def reduce_end(phase, copies):
        for copy in copies:
            copy.wait_recv()
        total = slots_ref[phase, 0]
        for n in range(1, len(copies) + 1):
            total = total + slots_ref[phase, n]
        return total

    row_id = lax.broadcasted_iota(jnp.int32, (T, T), 0)
    lane_id = lax.broadcasted_iota(jnp.int32, (T, T), 1)
    upper = row_id < R
    first_lanes = lane_id < R
    has_up, has_down = r > 0, r < size_r - 1
    has_left, has_right = c > 0, c < size_c - 1

    extrapolate(0, mask_ref[...], prev_ref[...])
    pl.semaphore_wait(barrier, len(everyone))
    sent = send_point(0)
    pending = list(sent)

    padded_ref[...] = jnp.zeros_like(padded_ref)
    taps_copy.wait()
    table_copy.wait()

    def spectrum(k, carry):
        for part in range(2):
            padded_ref[part, 0:KS, 0:KS] = taps_ref[k, part]
            xh, xl = split(padded_ref[part])
            y = mm(lanes(xh, xh, xl), rows(tab("wkh"), tab("wkl"), tab("wkh")))
            yh, yl = split(y)
            dh, dl = tab("dkh")[:, :KP], tab("dkl")[:, :KP]
            q = mm(dh, yh) + mm(dh, yl) + mm(dl, yh)
            hr_ref[k, :, part * T : (part + 1) * T] = q[:N, :T] + q[N:, T:]
            hi_ref[k, :, part * T : (part + 1) * T] = q[:N, T:] - q[N:, :T]
        return carry

    lax.fori_loop(0, K, spectrum, 0)

    previous = mask_ref[...]
    objective = []
    for t in range(ITERS):
        point = point_ref[t]
        slot = 2 * t
        for copy in sent:
            copy.wait_recv()
        zero = jnp.zeros((T, T), F32)
        rows_live = jnp.where(upper, has_down.astype(F32), has_up.astype(F32))
        lanes_live = jnp.where(first_lanes, has_right.astype(F32), has_left.astype(F32))
        below = ud_ref[slot] * rows_live
        beside = jnp.where(first_lanes, lr_ref[slot, 1], lr_ref[slot, 0]) * lanes_live
        corner = jnp.where(first_lanes, corner_ref[slot, 1], corner_ref[slot, 0]) * (rows_live * lanes_live)
        x = rows(lanes(point, beside), lanes(below, corner))

        strip = rows(x[N - 8 :], x[: T + 8])
        high_rows = strip.shape[0]
        step_down = pltpu.roll(strip, high_rows - 1, 0) - strip
        step_side = pltpu.roll(strip, N - 1, 1) - strip
        squared = step_down * step_down + step_side * step_side + EPS_TV
        inverse = lax.rsqrt(squared)
        flow_down = step_down * inverse
        flow_side = step_side * inverse
        from_up = pltpu.roll(flow_down, 1, 0)[8 : T + 8, :T]
        from_left = pltpu.roll(flow_side, 1, 1)[8 : T + 8, :T]
        from_up = jnp.where((row_id == 0) & (r == 0), zero, from_up)
        from_left = jnp.where((lane_id == 0) & (c == 0), zero, from_left)
        grad_tv = from_up + from_left - (flow_down + flow_side)[8 : T + 8, :T]
        length = (squared * inverse)[8 : T + 8, :T]

        xh, xl = split(x)
        a = mm(lanes(xh, xh, xl), rows(tab("wh"), tab("wl"), tab("wh")))
        ah, al = split(a)
        q = mm(lanes(tab("dh"), tab("dh"), tab("dl")), rows(ah, al, ah))
        mr = q[:N, :T] + q[N:, T:]
        mi = q[:N, T:] - q[N:, :T]
        gr_ref[...] = lanes(mr, mr)
        gi_ref[...] = lanes(mi, mi)

        def forward(k, total):
            m_r, m_i, h_r, h_i = gr_ref[...], gi_ref[...], hr_ref[k], hi_ref[k]
            p_r = m_r * h_r + m_i * h_i
            p_i = m_i * h_r - m_r * h_i
            plus = rows(p_r[:T] + p_r[T:], p_i[:T] + p_i[T:])
            minus = rows(p_r[:T] - p_r[T:], p_i[:T] - p_i[T:])
            bh, bl = split(plus)
            z_even = mm(lanes(tab("evenh"), tab("evenh"), tab("evenl")), rows(bh, bl, bh))
            bh, bl = split(minus)
            z_odd = mm(lanes(tab("oddh"), tab("oddh"), tab("oddl")), rows(bh, bl, bh))
            z = rows(
                lanes(z_even[:R, :T], z_even[R:, :T]),
                lanes(z_odd[:R, :T], z_odd[R:, :T]),
                lanes(z_even[:R, T:], z_even[R:, T:]),
                lanes(z_odd[:R, T:], z_odd[R:, T:]),
            )
            zh, zl = split(z)
            wi = lanes(tab("wih")[:, :T], tab("wil")[:, :T])
            e = mm(zh, wi)
            f = mm(zl, wi)
            e = (e[:, :T] + e[:, T:]) + (f[:, :T] + f[:, T:])
            field_ref[k] = e
            square = e * e
            return total + (square[:T] + square[T:])

        intensity = lax.fori_loop(0, K, forward, zero)
        wanted = rows(target_ref[pl.ds(0, R, stride=2), :], target_ref[pl.ds(1, R, stride=2), :])
        resist = 1.0 / (1.0 + jnp.exp(-SLOPE * (intensity - LEVEL)))
        miss = resist - wanted
        weight = 2.0 * miss * SLOPE * resist * (1.0 - resist)
        term = miss * miss + TV_WEIGHT * length + L1_WEIGHT * jnp.abs(point)
        goal_part[t] = jnp.sum(term.reshape(T // 8, 8, T), axis=0)

        gr_ref[...] = jnp.zeros_like(gr_ref)
        gi_ref[...] = jnp.zeros_like(gi_ref)
        weight2 = rows(weight, weight)

        def adjoint(k, carry):
            vh, vl = split(weight2 * field_ref[k])
            v = lanes(vh, vl)
            wh, wl = tab("wh")[:T], tab("wl")[:T]
            y = mm(v, rows(wh, wh)) + mm(v, rows(wl, wl))
            y_r = lanes(y[:T, :T], y[T:, :T])
            y_i = lanes(y[:T, T:], y[T:, T:])
            out = []
            for n in range(2):
                half = slice(n * R, (n + 1) * R)
                yh, yl = split(rows(y_r[half], y_i[half]))
                y2 = rows(yh, yl)
                bh = tab("bothh")[:, n * T : (n + 1) * T]
                bl = tab("bothl")[:, n * T : (n + 1) * T]
                out.append(mm(lanes(bh, bh), y2) + mm(lanes(bl, bl), y2))
            even, odd = out
            first = even + odd
            second = even - odd
            for n, s in enumerate((first, second)):
                at = slice(n * T, (n + 1) * T)
                s_r, s_i = s[:T], s[T:]
                h_r, h_i = hr_ref[k, at], hi_ref[k, at]
                gr_ref[at] += h_r * s_r - h_i * s_i
                gi_ref[at] += h_r * s_i + h_i * s_r
            return carry

        last = t == ITERS - 1
        reducing = None
        if last:
            line = lax.broadcasted_iota(jnp.int32, (8, T), 0)
            value = jnp.zeros((8, T), F32)
            for n in range(ITERS):
                value = jnp.where(line == n, jnp.sum(goal_part[n], axis=0, keepdims=True), value)
            reducing = reduce_start(0, value)
            pending += reducing
            lax.fori_loop(0, K // 2, adjoint, 0)
            reducing = reduce_start(1, reduce_end(0, reducing))
            pending += reducing
            lax.fori_loop(K // 2, K, adjoint, 0)
        else:
            lax.fori_loop(0, K, adjoint, 0)
        g = lanes(gr_ref[:, :T] + gr_ref[:, T:], gi_ref[:, :T] + gi_ref[:, T:])
        gh, gl = split(g)
        q = mm(lanes(tab("dh"), tab("dh"), tab("dl")), rows(gh, gl, gh))
        z = lanes(q[:N, :T] - q[N:, T:], q[:N, T:] + q[N:, :T])
        zh, zl = split(z)
        own_ref[t] = mm(lanes(zh, zh, zl), rows(tab("wih"), tab("wil"), tab("wih")))
        sent = send_gradient(t)
        pending += sent
        if last:
            reducing = reduce_start(2, reduce_end(1, reducing))
            pending += reducing
        for copy in sent:
            copy.wait_recv()
        slot = 2 * t + 1
        rows_live = jnp.where(upper, has_up.astype(F32), has_down.astype(F32))
        lanes_live = jnp.where(first_lanes, has_left.astype(F32), has_right.astype(F32))
        grad_data = own_ref[t, 0:T, 0:T] + ud_ref[slot] * rows_live
        beside = jnp.where(first_lanes, lr_ref[slot, 0], lr_ref[slot, 1])
        corner = jnp.where(first_lanes, corner_ref[slot, 0], corner_ref[slot, 1])
        grad_data = 2.0 * (grad_data + (beside + corner * rows_live) * lanes_live)
        updated = jnp.clip(
            point - STEP_SIZE * (grad_data + TV_WEIGHT * grad_tv) - STEP_SIZE * L1_WEIGHT, 0.0, 1.0
        )
        if last:
            next_ref[...] = updated
            total = reduce_end(2, reducing)
            scale = 1.0 / (size_r * size_c * T * T)
            for n in range(ITERS):
                goal_ref[n] = jnp.sum(total[n : n + 1]) * scale
        else:
            last_ref[...] = updated
            extrapolate(t + 1, updated, previous)
            previous = updated
            sent = send_point(t + 1)
            pending += sent
    for copy in pending:
        copy.wait_send()


def shards(size_r, size_c, mask, mask_prev, target, kernels, restart):
    vmem = pl.BlockSpec(memory_space=pltpu.VMEM)
    smem = pl.BlockSpec(memory_space=pltpu.SMEM)
    anywhere = pl.BlockSpec(memory_space=pl.ANY)
    low = min(8, size_r)
    widest = max(size_c, low, size_r // low)
    return pl.pallas_call(
        functools.partial(kernel, size_r, size_c),
        out_shape=(
            jax.ShapeDtypeStruct((T, T), F32),
            jax.ShapeDtypeStruct((T, T), F32),
            jax.ShapeDtypeStruct((ITERS,), F32),
        ),
        in_specs=[vmem, vmem, vmem, smem, anywhere, anywhere],
        out_specs=(vmem, vmem, smem),
        scratch_shapes=[
            pltpu.VMEM((K, 2, KS, KS), F32),
            pltpu.VMEM(TABLE.shape, BF16),
            pltpu.VMEM((2, KP, N), F32),
            pltpu.VMEM((K, N, N), F32),
            pltpu.VMEM((K, N, N), F32),
            pltpu.VMEM((K, N, T), F32),
            pltpu.VMEM((N, N), F32),
            pltpu.VMEM((N, N), F32),
            pltpu.VMEM((ITERS, T, T), F32),
            pltpu.VMEM((ITERS, N, N), F32),
            pltpu.VMEM((2 * ITERS, T, T), F32),
            pltpu.VMEM((2 * ITERS, 2, T, T), F32),
            pltpu.VMEM((2 * ITERS, 2, T, T), F32),
            pltpu.VMEM((ITERS, 8, T), F32),
            pltpu.VMEM((3, widest, 8, T), F32),
            pltpu.VMEM((3, 8, T), F32),
            pltpu.SemaphoreType.DMA((2,)),
            pltpu.SemaphoreType.DMA((2 * ITERS, 8)),
            pltpu.SemaphoreType.DMA((2 * ITERS, 8)),
            pltpu.SemaphoreType.DMA((3, widest)),
            pltpu.SemaphoreType.DMA((3, widest)),
        ],
        compiler_params=pltpu.CompilerParams(
            collective_id=0, has_side_effects=True, vmem_limit_bytes=48 * 1024 * 1024
        ),
        name="fista",
    )(mask, mask_prev, target, restart, kernels, jnp.asarray(TABLE))


def solution(mesh):
    in_specs = (P("row", "col"), P("row", "col"), P("row", "col"), P(), P(None, "row", "col"))
    out_specs = (P("row", "col"), P("row", "col"), P())
    body = functools.partial(shards, mesh.shape["row"], mesh.shape["col"])
    return jax.shard_map(body, mesh=mesh, in_specs=in_specs, out_specs=out_specs, check_vma=False)
```

time: 436 us -> 72.6 us (0.17); the launches traced: 429 us -> 71.2 us
  matrix products: 167 us -> 0 us
  blocking collectives: 95.7 us -> 0 us
  Pallas kernels: 0 us -> 66 us
  local copies, waits for them, and re-layouts: 55.7 us -> 4.51 us
  starting transfers between devices: 48.1 us -> 0 us
  waiting for transfers between devices: 34.8 us -> 0 us
  other arithmetic: 19.7 us -> 0 us
  between operations: 8.5 us -> 0.71 us
    dot_general x72 -> x0, matrix products: 167 us -> none  [multiply(): return jnp.matmul(left_arr, right_arr, precision=lax.Precision.HIGHEST)]
    psum x1 -> x0, blocking collectives: 95.7 us -> none  [shards(): lax.psum(local_term, ('row', 'col')) / (grid_rows * grid_cols)]
    pallas_call x0 -> x1, Pallas kernels: none -> 66 us  [shards(): pl.pallas_call(functools.partial(kernel, size_r, size_c), out_shape=(jax....]
    ppermute x16 -> x0, starting transfers between devices: 48.1 us -> none  [the longest x8 34.8 us: with_halo(): before = lax.ppermute(last, axis, up)]
    ppermute x16 -> x0, waiting for transfers between devices: 34.8 us -> none  [the longest x8 21.1 us: with_halo(): after = lax.ppermute(initial, axis, down)]
    slice x12 -> x0, local copies, waits for them, and re-layouts: 23.3 us -> none  [the longest x8 12.2 us: with_halo(): last = lax.slice_in_dim(x, length - width, length, axis=dim)]
    unnamed x80 -> x13, local copies, waits for them, and re-layouts: 21 us -> 4.51 us
    concatenate x10 -> x0, other arithmetic: 12.1 us -> none  [the longest x8 11.9 us: with_halo(): x = jnp.concatenate([before, x, after], axis=dim)]
  transfers between devices with their start and end apart: 16 -> 0, of which waited for: 9 -> 0; matrix products, arithmetic and copies ran while one was open for 23% -> 0% of each run, Pallas kernels for 0% -> 0%
where the time goes in v1:
time: 72.6 us; the launch traced here: 71.2 us
  Pallas kernels  66 us (91%)
  local copies, waits for them, and re-layouts  4.51 us (6%)
    pallas_call x1, Pallas kernels, shards(): pl.pallas_call(functools.partial(kernel, size_r, size_c), out_shape=(jax....  66 us
    unnamed x13, local copies, waits for them, and re-layouts  4.51 us

profile of v1, /device:TPU:1, one launch (start us, length us, event | category | flops | bytes accessed | tf_op | source)
XLA Modules:
  0.0 71.2 jit_solution(777486734766716487)
XLA Ops:
  0.6 0.0 copy-start
  0.6 0.0 copy-start.3
  0.7 0.0 copy-start.2
  0.7 0.0 copy-start.1
  0.7 0.9 %copy.9.restart_ref = s32[2,1,1]{2,1,0:T(1,128)S(1)} copy(s32[2,1,1]{0,2,1:T(1,128)} %param.10) | data formatting | bytes 16 | tf_op args[4]
  1.6 1.8 %copy.10.taps_hbm = f32[8,2,129,129]{3,2,1,0:T(8,128)S(1)} copy(f32[8,2,129,129]{3,1,2,0:T(2,128)} %param.9) | data formatting | bytes 2130048 | tf_op args[3]
  3.4 0.0 copy-done
  3.4 0.0 copy-done.3
  3.4 0.0 copy-done.2
  3.4 0.0 copy-done.1
  3.4 66.0 %fista.1 = (f32[128,128]{1,0:T(8,128)S(1)}, f32[128,128]{1,0:T(8,128)S(1)}, f32[2]{0:T(128)S(1)}) custom-call(f32[128,128]{1,0:T(8,128)S(1)} %copy-done.1, f32[128,128]{1,0:T(8,128)S(1)} %copy-done.2, f32[128,128]{1,0:T(8,128)S(1)} %copy-done.3, s32[2,1,1]{2,1,0:T(1,128)S(1)} %copy.9.restart_ref, f32[8,2,129,129]{3,2,1,0:T(8,128)S(1)} %copy.10.taps_hbm, ...), custom_call_target="tpu_custom_call" | custom-call | tf_op jit(solution)/shard_map/fista/pallas_call | solution.py:422
  69.5 0.6 copy.14
  70.1 0.6 copy.15
  70.7 0.5 copy.16
Async XLA Ops:
  0.6 2.8 %copy-start = (bf16[4608,256]{1,0:T(8,128)(2,1)S(1)}, bf16[4608,256]{1,0:T(8,128)(2,1)}, u32[]{:S(2)}) copy-start(bf16[4608,256]{1,0:T(8,128)(2,1)} %constant.2.clone.table_hbm) | copy-start | bytes 7077892
  0.6 2.8 %copy-start.3 = (f32[128,128]{1,0:T(8,128)S(1)}, f32[128,128]{1,0:T(8,128)}, u32[]{:S(2)}) copy-start(f32[128,128]{1,0:T(8,128)} %target_ref.1) | copy-start | bytes 196612
  0.7 2.8 %copy-start.2 = (f32[128,128]{1,0:T(8,128)S(1)}, f32[128,128]{1,0:T(8,128)}, u32[]{:S(2)}) copy-start(f32[128,128]{1,0:T(8,128)} %prev_ref.1) | copy-start | bytes 196612
  0.7 2.8 %copy-start.1 = (f32[128,128]{1,0:T(8,128)S(1)}, f32[128,128]{1,0:T(8,128)}, u32[]{:S(2)}) copy-start(f32[128,128]{1,0:T(8,128)} %mask_ref.1) | copy-start | bytes 196612

commit v2 on v1

--- a/solution.py
+++ b/solution.py
@@ -115,8 +115,10 @@
     point_ref,
     own_ref,
     ud_ref,
-    lr_ref,
+    side_ref,
     corner_ref,
+    side_out,
+    corner_out,
     goal_part,
     slots_ref,
     sums_ref,
@@ -128,9 +130,11 @@
 ):
     r = lax.axis_index("row")
     c = lax.axis_index("col")
-    near = []
-    for dr, dc in ((1, 0), (-1, 0), (0, 1), (0, -1), (1, 1), (1, -1), (-1, 1), (-1, -1)):
-        near.append((lax.rem(r + dr + size_r, size_r), lax.rem(c + dc + size_c, size_c)))
+    near = {}
+    for dr in (-1, 0, 1):
+        for dc in (-1, 0, 1):
+            if dr or dc:
+                near[dr, dc] = (lax.rem(r + dr + size_r, size_r), lax.rem(c + dc + size_c, size_c))
     low = min(8, size_r)
     high = size_r // low
     r_high, r_low = r // low, lax.rem(r, low)
@@ -148,58 +152,65 @@
     table_copy.start()
     taps_copy.start()
     barrier = pltpu.get_barrier_semaphore()
-    everyone = near + [peer for _, peers in groups for peer in peers]
+    everyone = list(near.values()) + [peer for _, peers in groups for peer in peers]
     for peer in everyone:
         pl.semaphore_signal(barrier, inc=1, device_id=peer, device_id_type=MESH)
 
     def extrapolate(t, current, previous):
         momentum = (t + PRIOR_STEPS - 1.0) / (t + PRIOR_STEPS + 2.0)
-        keep = 1.0 - restart_ref[t, 0, 0].astype(F32)
-        point_ref[t] = current + keep * momentum * (current - previous)
-
-    def exchange(slot, down, up, side, corner_down, corner_up):
+        keep = 1.0 - restart_ref[0, 0, t].astype(F32)
+        point = current + keep * momentum * (current - previous)
+        point_ref[t] = point
+        return point
+
+    def exchange(slot, sign, beyond, beside, corner):
+        side_out[slot, 0], side_out[slot, 1] = pack(beside)
+        for h in range(2):
+            corner_out[slot, h, 0], corner_out[slot, h, 1] = pack(corner[h * R : (h + 1) * R])
+        pieces = []
+        ways = (-sign, sign)
+        for h in range(2):
+            for p in range(2):
+                pieces.append((ways[h], ways[p], corner_out.at[slot, h, p], corner_ref.at[slot, h, p]))
+        for h in range(2):
+            half = pl.ds(h * R, R)
+            pieces.append((ways[h], 0, beyond.at[half], ud_ref.at[slot, half]))
+        for p in range(2):
+            pieces.append((0, ways[p], side_out.at[slot, p], side_ref.at[slot, p]))
         copies = []
-        pieces = (
-            (down[0], ud_ref.at[slot, down[1]]),
-            (up[0], ud_ref.at[slot, up[1]]),
-            (side, lr_ref.at[slot, 0]),
-            (side, lr_ref.at[slot, 1]),
-            (corner_down, corner_ref.at[slot, 0, down[1]]),
-            (corner_down, corner_ref.at[slot, 1, down[1]]),
-            (corner_up, corner_ref.at[slot, 0, up[1]]),
-            (corner_up, corner_ref.at[slot, 1, up[1]]),
-        )
-        for n, (source, target) in enumerate(pieces):
+        for n, (dr, dc, source, target) in enumerate(pieces):
             copy = pltpu.make_async_remote_copy(
                 src_ref=source,
                 dst_ref=target,
                 send_sem=send_sem.at[slot, n],
                 recv_sem=recv_sem.at[slot, n],
-                device_id=near[n],
+                device_id=near[dr, dc],
                 device_id_type=MESH,
             )
             copy.start()
             copies.append(copy)
         return copies
 
-    top, bottom = pl.ds(0, R), pl.ds(R, R)
-
-    def send_point(t):
-        ref = point_ref.at[t]
-        return exchange(2 * t, (ref.at[bottom], bottom), (ref.at[top], top), ref, ref.at[bottom], ref.at[top])
-
-    def send_gradient(t):
-        down, up = pl.ds(T, R), pl.ds(T + R, R)
-        left_lanes, right_lanes = pl.ds(0, T), pl.ds(T, T)
-        ref = own_ref.at[t]
-        return exchange(
-            2 * t + 1,
-            (ref.at[down, left_lanes], top),
-            (ref.at[up, left_lanes], bottom),
-            ref.at[pl.ds(0, T), right_lanes],
-            ref.at[down, right_lanes],
-            ref.at[up, right_lanes],
-        )
+    def pack(block):
+        half = block.shape[0] // 2
+        turned = pltpu.roll(block, R, 1)
+        first = first_lanes[:half]
+        return jnp.where(first, block[:half], turned[half:]), jnp.where(first, turned[:half], block[half:])
+
+    def unpack(low, high):
+        first = first_lanes[: low.shape[0]]
+        return rows(jnp.where(first, low, pltpu.roll(high, R, 1)), jnp.where(first, pltpu.roll(low, R, 1), high))
+
+    def arrived(slot):
+        corner = rows(*(unpack(corner_ref[slot, h, 0], corner_ref[slot, h, 1]) for h in range(2)))
+        return ud_ref[slot], unpack(side_ref[slot, 0], side_ref[slot, 1]), corner
+
+    def send_point(t, point):
+        return exchange(2 * t, 1, point_ref.at[t], point, point)
+
+    def send_gradient(t, g):
+        own_ref[t] = g[T:, :T]
+        return exchange(2 * t + 1, -1, own_ref.at[t], g[:T, T:], g[T:, T:])
 
     def reduce_start(phase, value):
         me, peers = groups[phase]
@@ -234,9 +245,9 @@
     has_up, has_down = r > 0, r < size_r - 1
     has_left, has_right = c > 0, c < size_c - 1
 
-    extrapolate(0, mask_ref[...], prev_ref[...])
+    point = extrapolate(0, mask_ref[...], prev_ref[...])
     pl.semaphore_wait(barrier, len(everyone))
-    sent = send_point(0)
+    sent = send_point(0, point)
     pending = list(sent)
 
     padded_ref[...] = jnp.zeros_like(padded_ref)
@@ -255,21 +266,20 @@
             hi_ref[k, :, part * T : (part + 1) * T] = q[:N, T:] - q[N:, :T]
         return carry
 
-    lax.fori_loop(0, K, spectrum, 0)
+    lax.fori_loop(0, K, spectrum, 0, unroll=True)
 
     previous = mask_ref[...]
     objective = []
     for t in range(ITERS):
-        point = point_ref[t]
-        slot = 2 * t
         for copy in sent:
             copy.wait_recv()
         zero = jnp.zeros((T, T), F32)
         rows_live = jnp.where(upper, has_down.astype(F32), has_up.astype(F32))
         lanes_live = jnp.where(first_lanes, has_right.astype(F32), has_left.astype(F32))
-        below = ud_ref[slot] * rows_live
-        beside = jnp.where(first_lanes, lr_ref[slot, 1], lr_ref[slot, 0]) * lanes_live
-        corner = jnp.where(first_lanes, corner_ref[slot, 1], corner_ref[slot, 0]) * (rows_live * lanes_live)
+        below, beside, corner = arrived(2 * t)
+        below = below * rows_live
+        beside = beside * lanes_live
+        corner = corner * (rows_live * lanes_live)
         x = rows(lanes(point, beside), lanes(below, corner))
 
         strip = rows(x[N - 8 :], x[: T + 8])
@@ -321,7 +331,7 @@
             square = e * e
             return total + (square[:T] + square[T:])
 
-        intensity = lax.fori_loop(0, K, forward, zero)
+        intensity = lax.fori_loop(0, K, forward, zero, unroll=True)
         wanted = rows(target_ref[pl.ds(0, R, stride=2), :], target_ref[pl.ds(1, R, stride=2), :])
         resist = 1.0 / (1.0 + jnp.exp(-SLOPE * (intensity - LEVEL)))
         miss = resist - wanted
@@ -368,32 +378,29 @@
                 value = jnp.where(line == n, jnp.sum(goal_part[n], axis=0, keepdims=True), value)
             reducing = reduce_start(0, value)
             pending += reducing
-            lax.fori_loop(0, K // 2, adjoint, 0)
+            lax.fori_loop(0, K // 2, adjoint, 0, unroll=True)
             reducing = reduce_start(1, reduce_end(0, reducing))
             pending += reducing
-            lax.fori_loop(K // 2, K, adjoint, 0)
+            lax.fori_loop(K // 2, K, adjoint, 0, unroll=True)
         else:
-            lax.fori_loop(0, K, adjoint, 0)
+            lax.fori_loop(0, K, adjoint, 0, unroll=True)
         g = lanes(gr_ref[:, :T] + gr_ref[:, T:], gi_ref[:, :T] + gi_ref[:, T:])
         gh, gl = split(g)
         q = mm(lanes(tab("dh"), tab("dh"), tab("dl")), rows(gh, gl, gh))
         z = lanes(q[:N, :T] - q[N:, T:], q[:N, T:] + q[N:, :T])
         zh, zl = split(z)
-        own_ref[t] = mm(lanes(zh, zh, zl), rows(tab("wih"), tab("wil"), tab("wih")))
-        sent = send_gradient(t)
+        g = mm(lanes(zh, zh, zl), rows(tab("wih"), tab("wil"), tab("wih")))
+        sent = send_gradient(t, g)
         pending += sent
         if last:
             reducing = reduce_start(2, reduce_end(1, reducing))
             pending += reducing
         for copy in sent:
             copy.wait_recv()
-        slot = 2 * t + 1
         rows_live = jnp.where(upper, has_up.astype(F32), has_down.astype(F32))
         lanes_live = jnp.where(first_lanes, has_left.astype(F32), has_right.astype(F32))
-        grad_data = own_ref[t, 0:T, 0:T] + ud_ref[slot] * rows_live
-        beside = jnp.where(first_lanes, lr_ref[slot, 0], lr_ref[slot, 1])
-        corner = jnp.where(first_lanes, corner_ref[slot, 0], corner_ref[slot, 1])
-        grad_data = 2.0 * (grad_data + (beside + corner * rows_live) * lanes_live)
+        below, beside, corner = arrived(2 * t + 1)
+        grad_data = 2.0 * (g[:T, :T] + below * rows_live + (beside + corner * rows_live) * lanes_live)
         updated = jnp.clip(
             point - STEP_SIZE * (grad_data + TV_WEIGHT * grad_tv) - STEP_SIZE * L1_WEIGHT, 0.0, 1.0
         )
@@ -405,9 +412,9 @@
                 goal_ref[n] = jnp.sum(total[n : n + 1]) * scale
         else:
             last_ref[...] = updated
-            extrapolate(t + 1, updated, previous)
+            point = extrapolate(t + 1, updated, previous)
             previous = updated
-            sent = send_point(t + 1)
+            sent = send_point(t + 1, point)
             pending += sent
     for copy in pending:
         copy.wait_send()
@@ -438,10 +445,12 @@
             pltpu.VMEM((N, N), F32),
             pltpu.VMEM((N, N), F32),
             pltpu.VMEM((ITERS, T, T), F32),
-            pltpu.VMEM((ITERS, N, N), F32),
+            pltpu.VMEM((ITERS, T, T), F32),
             pltpu.VMEM((2 * ITERS, T, T), F32),
-            pltpu.VMEM((2 * ITERS, 2, T, T), F32),
-            pltpu.VMEM((2 * ITERS, 2, T, T), F32),
+            pltpu.VMEM((2 * ITERS, 2, R, T), F32),
+            pltpu.VMEM((2 * ITERS, 2, 2, R // 2, T), F32),
+            pltpu.VMEM((2 * ITERS, 2, R, T), F32),
+            pltpu.VMEM((2 * ITERS, 2, 2, R // 2, T), F32),
             pltpu.VMEM((ITERS, 8, T), F32),
             pltpu.VMEM((3, widest, 8, T), F32),
             pltpu.VMEM((3, 8, T), F32),
@@ -455,7 +464,7 @@
             collective_id=0, has_side_effects=True, vmem_limit_bytes=48 * 1024 * 1024
         ),
         name="fista",
-    )(mask, mask_prev, target, restart, kernels, jnp.asarray(TABLE))
+    )(mask, mask_prev, target, jnp.transpose(restart, (1, 2, 0)), kernels, jnp.asarray(TABLE))
 
 
 def solution(mesh):

time: 72.6 us -> 61.2 us (0.84); the launches traced: 71.2 us -> 61.2 us
  Pallas kernels: 66 us -> 56.4 us
    pallas_call x1, Pallas kernels: 66 us -> 56.4 us  [shards(): pl.pallas_call(functools.partial(kernel, size_r, size_c), out_shape=(jax....]
    unnamed x13 -> x14, local copies, waits for them, and re-layouts: 4.51 us -> 4.04 us
where the time goes in v2:
time: 61.2 us
  Pallas kernels  56.4 us (92%)
  local copies, waits for them, and re-layouts  4.04 us (7%)
  between operations  0.69 us (1%)
    pallas_call x1, Pallas kernels, shards(): pl.pallas_call(functools.partial(kernel, size_r, size_c), out_shape=(jax....  56.4 us
    unnamed x14, local copies, waits for them, and re-layouts  4.04 us

profile of v2, /device:TPU:1, one launch (start us, length us, event | category | flops | bytes accessed | tf_op | source)
XLA Modules:
  0.0 61.2 jit_solution(11776079106194866029)
XLA Ops:
  0.6 0.0 copy-start
  0.6 0.0 copy-start.4
  0.7 0.0 copy-start.3
  0.7 0.0 copy-start.2
  0.7 0.0 copy-start.1
  0.7 2.0 %copy.9.taps_hbm = f32[8,2,129,129]{3,2,1,0:T(8,128)S(1)} copy(f32[8,2,129,129]{3,1,2,0:T(2,128)} %param.9) | data formatting | bytes 2130048 | tf_op args[3]
  2.7 0.3 copy-done
  2.9 0.0 copy-done.4
  2.9 0.0 copy-done.3
  2.9 0.0 copy-done.2
  2.9 0.0 copy-done.1
  2.9 56.4 %fista.1 = (f32[128,128]{1,0:T(8,128)S(1)}, f32[128,128]{1,0:T(8,128)S(1)}, f32[2]{0:T(128)S(1)}) custom-call(f32[128,128]{1,0:T(8,128)S(1)} %copy-done.1, f32[128,128]{1,0:T(8,128)S(1)} %copy-done.2, f32[128,128]{1,0:T(8,128)S(1)} %copy-done.3, s32[1,1,2]{2,1,0:T(1,128)S(1)} %bitcast.1, f32[8,2,129,129]{3,2,1,0:T(8,128)S(1)} %copy.9.taps_hbm, ...), custom_call_target="tpu_custom_call" | custom-call | tf_op jit(solution)/shard_map/fista/pallas_call | solution.py:429
  59.4 0.6 %copy.13 = f32[128,128]{1,0:T(8,128)} copy(f32[128,128]{1,0:T(8,128)S(1)} %get-tuple-element.6) | data formatting | bytes 131072
  60.0 0.6 %copy.14 = f32[128,128]{1,0:T(8,128)} copy(f32[128,128]{1,0:T(8,128)S(1)} %get-tuple-element.7) | data formatting | bytes 131072
  60.6 0.5 copy.15
Async XLA Ops:
  0.6 2.3 %copy-start = (bf16[4608,256]{1,0:T(8,128)(2,1)S(1)}, bf16[4608,256]{1,0:T(8,128)(2,1)}, u32[]{:S(2)}) copy-start(bf16[4608,256]{1,0:T(8,128)(2,1)} %constant.2.clone.table_hbm) | copy-start | bytes 7077892
  0.6 2.3 %copy-start.4 = (s32[2,1,1]{0,2,1:T(1,128)S(1)}, s32[2,1,1]{0,2,1:T(1,128)}, u32[]{:S(2)}) copy-start(s32[2,1,1]{0,2,1:T(1,128)} %param.10) | copy-start | bytes 28
  0.7 2.3 %copy-start.3 = (f32[128,128]{1,0:T(8,128)S(1)}, f32[128,128]{1,0:T(8,128)}, u32[]{:S(2)}) copy-start(f32[128,128]{1,0:T(8,128)} %target_ref.1) | copy-start | bytes 196612
  0.7 2.3 %copy-start.2 = (f32[128,128]{1,0:T(8,128)S(1)}, f32[128,128]{1,0:T(8,128)}, u32[]{:S(2)}) copy-start(f32[128,128]{1,0:T(8,128)} %prev_ref.1) | copy-start | bytes 196612
  0.7 2.3 %copy-start.1 = (f32[128,128]{1,0:T(8,128)S(1)}, f32[128,128]{1,0:T(8,128)}, u32[]{:S(2)}) copy-start(f32[128,128]{1,0:T(8,128)} %mask_ref.1) | copy-start | bytes 196612

commit v3 on v2

--- a/solution.py
+++ b/solution.py
@@ -73,6 +73,13 @@
 
 
 PLACE, TABLE = tables()
+
+
+def factors(size_r, size_c):
+    core = math.gcd(size_r, 2)
+    x = math.gcd(size_r // core, 4)
+    y = math.gcd(size_c, 4)
+    return (size_r // (core * x), x, core), (size_c // y, y)
 
 
 def split(x):
@@ -135,13 +142,31 @@
         for dc in (-1, 0, 1):
             if dr or dc:
                 near[dr, dc] = (lax.rem(r + dr + size_r, size_r), lax.rem(c + dc + size_c, size_c))
-    low = min(8, size_r)
-    high = size_r // low
-    r_high, r_low = r // low, lax.rem(r, low)
+    rows_by, cols_by = factors(size_r, size_c)
+    z_high, x, core = r // (rows_by[1] * rows_by[2]), lax.rem(r // rows_by[2], rows_by[1]), lax.rem(r, rows_by[2])
+    z_low, y = c // cols_by[1], lax.rem(c, cols_by[1])
+
+    def device(z_high, x, core, z_low, y):
+        return (z_high * rows_by[1] + x) * rows_by[2] + core, z_low * cols_by[1] + y
+
     groups = []
-    groups.append((c, [(r, lax.rem(c + d, size_c)) for d in range(1, size_c)]))
-    groups.append((r_low, [(r_high * low + lax.rem(r_low + d, low), c) for d in range(1, low)]))
-    groups.append((r_high, [(lax.rem(r_high + d, high) * low + r_low, c) for d in range(1, high)]))
+    peers = []
+    for i in range(rows_by[1]):
+        for j in range(cols_by[1]):
+            if i or j:
+                peers.append(device(z_high, lax.rem(x + i, rows_by[1]), core, z_low, lax.rem(y + j, cols_by[1])))
+    groups.append((x * cols_by[1] + y, peers))
+    peers = []
+    for i in range(rows_by[0]):
+        for j in range(cols_by[0]):
+            for k in range(rows_by[2]):
+                if i or j or k:
+                    peers.append(
+                        device(
+                            lax.rem(z_high + i, rows_by[0]), x, lax.rem(core + k, rows_by[2]), lax.rem(z_low + j, cols_by[0]), y
+                        )
+                    )
+    groups.append(((z_high * cols_by[0] + z_low) * rows_by[2] + core, peers))
 
     def tab(name):
         first, end = PLACE[name]
@@ -256,7 +281,7 @@
 
     def spectrum(k, carry):
         for part in range(2):
-            padded_ref[part, 0:KS, 0:KS] = taps_ref[k, part]
+            padded_ref[part, 0:KS, 0:KS] = taps_ref[k, :, part, :]
             xh, xl = split(padded_ref[part])
             y = mm(lanes(xh, xh, xl), rows(tab("wkh"), tab("wkl"), tab("wkh")))
             yh, yl = split(y)
@@ -378,12 +403,7 @@
                 value = jnp.where(line == n, jnp.sum(goal_part[n], axis=0, keepdims=True), value)
             reducing = reduce_start(0, value)
             pending += reducing
-            lax.fori_loop(0, K // 2, adjoint, 0, unroll=True)
-            reducing = reduce_start(1, reduce_end(0, reducing))
-            pending += reducing
-            lax.fori_loop(K // 2, K, adjoint, 0, unroll=True)
-        else:
-            lax.fori_loop(0, K, adjoint, 0, unroll=True)
+        lax.fori_loop(0, K, adjoint, 0, unroll=True)
         g = lanes(gr_ref[:, :T] + gr_ref[:, T:], gi_ref[:, :T] + gi_ref[:, T:])
         gh, gl = split(g)
         q = mm(lanes(tab("dh"), tab("dh"), tab("dl")), rows(gh, gl, gh))
@@ -393,7 +413,7 @@
         sent = send_gradient(t, g)
         pending += sent
         if last:
-            reducing = reduce_start(2, reduce_end(1, reducing))
+            reducing = reduce_start(1, reduce_end(0, reducing))
             pending += reducing
         for copy in sent:
             copy.wait_recv()
@@ -406,7 +426,7 @@
         )
         if last:
             next_ref[...] = updated
-            total = reduce_end(2, reducing)
+            total = reduce_end(1, reducing)
             scale = 1.0 / (size_r * size_c * T * T)
             for n in range(ITERS):
                 goal_ref[n] = jnp.sum(total[n : n + 1]) * scale
@@ -423,10 +443,10 @@
 def shards(size_r, size_c, mask, mask_prev, target, kernels, restart):
     vmem = pl.BlockSpec(memory_space=pltpu.VMEM)
     smem = pl.BlockSpec(memory_space=pltpu.SMEM)
-    anywhere = pl.BlockSpec(memory_space=pl.ANY)
-    low = min(8, size_r)
-    widest = max(size_c, low, size_r // low)
-    return pl.pallas_call(
+    anywhere = pl.BlockSpec(memory_space=pltpu.HBM)
+    rows_by, cols_by = factors(size_r, size_c)
+    widest = max(rows_by[1] * cols_by[1], rows_by[0] * cols_by[0] * rows_by[2])
+    results = pl.pallas_call(
         functools.partial(kernel, size_r, size_c),
         out_shape=(
             jax.ShapeDtypeStruct((T, T), F32),
@@ -436,7 +456,7 @@
         in_specs=[vmem, vmem, vmem, smem, anywhere, anywhere],
         out_specs=(vmem, vmem, smem),
         scratch_shapes=[
-            pltpu.VMEM((K, 2, KS, KS), F32),
+            pltpu.VMEM((K, KS, 2, KS), F32),
             pltpu.VMEM(TABLE.shape, BF16),
             pltpu.VMEM((2, KP, N), F32),
             pltpu.VMEM((K, N, N), F32),
@@ -452,19 +472,36 @@
             pltpu.VMEM((2 * ITERS, 2, R, T), F32),
             pltpu.VMEM((2 * ITERS, 2, 2, R // 2, T), F32),
             pltpu.VMEM((ITERS, 8, T), F32),
-            pltpu.VMEM((3, widest, 8, T), F32),
-            pltpu.VMEM((3, 8, T), F32),
+            pltpu.VMEM((2, widest, 8, T), F32),
+            pltpu.VMEM((2, 8, T), F32),
             pltpu.SemaphoreType.DMA((2,)),
             pltpu.SemaphoreType.DMA((2 * ITERS, 8)),
             pltpu.SemaphoreType.DMA((2 * ITERS, 8)),
-            pltpu.SemaphoreType.DMA((3, widest)),
-            pltpu.SemaphoreType.DMA((3, widest)),
+            pltpu.SemaphoreType.DMA((2, widest)),
+            pltpu.SemaphoreType.DMA((2, widest)),
         ],
         compiler_params=pltpu.CompilerParams(
-            collective_id=0, has_side_effects=True, vmem_limit_bytes=48 * 1024 * 1024
+            collective_id=0, has_side_effects=True, vmem_limit_bytes=62 * 1024 * 1024
         ),
         name="fista",
-    )(mask, mask_prev, target, jnp.transpose(restart, (1, 2, 0)), kernels, jnp.asarray(TABLE))
+    )(mask, mask_prev, target, jnp.transpose(restart, (1, 2, 0)), jnp.transpose(kernels, (0, 2, 1, 3)), jnp.asarray(TABLE))
+    return pl.pallas_call(
+        store,
+        out_shape=tuple(jax.ShapeDtypeStruct(x.shape, x.dtype) for x in results),
+        in_specs=[vmem, vmem, vmem],
+        out_specs=(anywhere, anywhere, anywhere),
+        scratch_shapes=[pltpu.SemaphoreType.DMA((3,))],
+        name="store",
+    )(*results)
+
+
+def store(a_ref, b_ref, c_ref, next_ref, last_ref, goal_ref, sems):
+    pairs = ((a_ref, next_ref), (b_ref, last_ref), (c_ref, goal_ref))
+    copies = [pltpu.make_async_copy(x, y, sems.at[n]) for n, (x, y) in enumerate(pairs)]
+    for copy in copies:
+        copy.start()
+    for copy in copies:
+        copy.wait()
 
 
 def solution(mesh):

time: 61.2 us -> 58.2 us (0.951)
  local copies, waits for them, and re-layouts: 4.04 us -> 0 us
  Pallas kernels: 56.4 us -> 57.3 us
    unnamed x14 -> x0, local copies, waits for them, and re-layouts: 4.04 us -> none
    pallas_call x0 -> x1, Pallas kernels: none -> 1.55 us  [shards(): pl.pallas_call(store, out_shape=tuple((jax.ShapeDtypeStruct(x.shape, x.dt...]
    pallas_call x1, Pallas kernels: 56.4 us -> 55.7 us  [shards(): pl.pallas_call(functools.partial(kernel, size_r, size_c), out_shape=(jax....]
where the time goes in v3:
time: 58.2 us; the launch traced here: 58.1 us
  Pallas kernels  57.3 us (98%)
  between operations  0.8 us (1%)
    pallas_call x1, Pallas kernels, shards(): pl.pallas_call(functools.partial(kernel, size_r, size_c), out_shape=(jax....  55.7 us
    pallas_call x1, Pallas kernels, shards(): pl.pallas_call(store, out_shape=tuple((jax.ShapeDtypeStruct(x.shape, x.dt...  1.55 us

profile of v3, /device:TPU:1, one launch (start us, length us, event | category | flops | bytes accessed | tf_op | source)
XLA Modules:
  0.0 58.1 jit_solution(16272541373939176831)
XLA Ops:
  0.6 55.7 %fista.1 = (f32[128,128]{1,0:T(8,128)}, f32[128,128]{1,0:T(8,128)}, f32[2]{0:T(128)}) custom-call(f32[128,128]{1,0:T(8,128)} %mask_ref.1, f32[128,128]{1,0:T(8,128)} %prev_ref.1, f32[128,128]{1,0:T(8,128)} %target_ref.1, s32[1,1,2]{2,1,0:T(1,128)} %bitcast.3, f32[8,129,2,129]{3,2,1,0:T(2,128)} %bitcast.2, bf16[4608,256]{1,0:T(8,128)(2,1)} %constant.2.clone.table_hbm), custom_call_target="tpu_custom_call" | custom-call | tf_op jit(solution)/shard_map/fista/pallas_call | solution.py:449
  56.3 1.6 %store.1 = (f32[128,128]{1,0:T(8,128)}, f32[128,128]{1,0:T(8,128)}, f32[2]{0:T(128)}) custom-call(f32[128,128]{1,0:T(8,128)} %get-tuple-element.6.a_ref, f32[128,128]{1,0:T(8,128)} %get-tuple-element.7.b_ref, f32[2]{0:T(128)} %get-tuple-element.8.c_ref), custom_call_target="tpu_custom_call" | custom-call | tf_op jit(solution)/shard_map/store/pallas_call | solution.py:488

commit v4 on v3

--- a/solution.py
+++ b/solution.py
@@ -25,6 +25,7 @@
 KP = 144
 K = 8
 R = 64
+CH = 16
 MESH = pl.DeviceIdType.MESH
 F32 = jnp.float32
 BF16 = jnp.bfloat16
@@ -102,15 +103,21 @@
 def kernel(
     size_r,
     size_c,
+    mask_hbm,
+    prev_hbm,
+    target_hbm,
+    restart_hbm,
+    taps_hbm,
+    table_hbm,
+    next_hbm,
+    last_hbm,
+    goal_ref,
+    next_ref,
+    last_ref,
     mask_ref,
     prev_ref,
     target_ref,
     restart_ref,
-    taps_hbm,
-    table_hbm,
-    next_ref,
-    last_ref,
-    goal_ref,
     taps_ref,
     table_ref,
     padded_ref,
@@ -121,6 +128,11 @@
     gi_ref,
     point_ref,
     own_ref,
+    b_ref,
+    z_ref,
+    v_ref,
+    y_ref,
+    m_ref,
     ud_ref,
     side_ref,
     corner_ref,
@@ -172,14 +184,34 @@
         first, end = PLACE[name]
         return table_ref[first:end, :]
 
-    taps_copy = pltpu.make_async_copy(taps_hbm, taps_ref, local_sem.at[0])
-    table_copy = pltpu.make_async_copy(table_hbm, table_ref, local_sem.at[1])
-    table_copy.start()
-    taps_copy.start()
+    loads = []
+    for n, (source, target) in enumerate(
+        (
+            (mask_hbm, mask_ref),
+            (prev_hbm, prev_ref),
+            (restart_hbm, restart_ref),
+            (table_hbm, table_ref),
+            (taps_hbm, taps_ref),
+            (target_hbm, target_ref),
+        )
+    ):
+        copy = pltpu.make_async_copy(source, target, local_sem.at[n])
+        loads.append(copy)
+    for copy in loads[:3]:
+        copy.start()
     barrier = pltpu.get_barrier_semaphore()
     everyone = list(near.values()) + [peer for _, peers in groups for peer in peers]
     for peer in everyone:
         pl.semaphore_signal(barrier, inc=1, device_id=peer, device_id_type=MESH)
+    for copy in loads[3:]:
+        copy.start()
+
+    stored = []
+
+    def put(n, source, target):
+        copy = pltpu.make_async_copy(source, target, local_sem.at[6 + n])
+        copy.start()
+        stored.append(copy)
 
     def extrapolate(t, current, previous):
         momentum = (t + PRIOR_STEPS - 1.0) / (t + PRIOR_STEPS + 2.0)
@@ -270,14 +302,16 @@
     has_up, has_down = r > 0, r < size_r - 1
     has_left, has_right = c > 0, c < size_c - 1
 
+    for copy in loads[:3]:
+        copy.wait()
     point = extrapolate(0, mask_ref[...], prev_ref[...])
     pl.semaphore_wait(barrier, len(everyone))
     sent = send_point(0, point)
     pending = list(sent)
 
     padded_ref[...] = jnp.zeros_like(padded_ref)
-    taps_copy.wait()
-    table_copy.wait()
+    for copy in loads[3:]:
+        copy.wait()
 
     def spectrum(k, carry):
         for part in range(2):
@@ -328,35 +362,47 @@
         q = mm(lanes(tab("dh"), tab("dh"), tab("dl")), rows(ah, al, ah))
         mr = q[:N, :T] + q[N:, T:]
         mi = q[:N, T:] - q[N:, :T]
-        gr_ref[...] = lanes(mr, mr)
-        gi_ref[...] = lanes(mi, mi)
-
-        def forward(k, total):
-            m_r, m_i, h_r, h_i = gr_ref[...], gi_ref[...], hr_ref[k], hi_ref[k]
-            p_r = m_r * h_r + m_i * h_i
-            p_i = m_i * h_r - m_r * h_i
-            plus = rows(p_r[:T] + p_r[T:], p_i[:T] + p_i[T:])
-            minus = rows(p_r[:T] - p_r[T:], p_i[:T] - p_i[T:])
-            bh, bl = split(plus)
-            z_even = mm(lanes(tab("evenh"), tab("evenh"), tab("evenl")), rows(bh, bl, bh))
-            bh, bl = split(minus)
-            z_odd = mm(lanes(tab("oddh"), tab("oddh"), tab("oddl")), rows(bh, bl, bh))
-            z = rows(
-                lanes(z_even[:R, :T], z_even[R:, :T]),
-                lanes(z_odd[:R, :T], z_odd[R:, :T]),
-                lanes(z_even[:R, T:], z_even[R:, T:]),
-                lanes(z_odd[:R, T:], z_odd[R:, T:]),
-            )
-            zh, zl = split(z)
+        m_ref[0], m_ref[1] = mr, mi
+
+        def spread(k):
+            for i in range(0, T, CH):
+                parts = []
+                for at in (slice(i, i + CH), slice(T + i, T + i + CH)):
+                    m_r, m_i = m_ref[0, at], m_ref[1, at]
+                    m_r, m_i = lanes(m_r, m_r), lanes(m_i, m_i)
+                    h_r, h_i = hr_ref[k, at], hi_ref[k, at]
+                    parts.append((m_r * h_r + m_i * h_i, m_i * h_r - m_r * h_i))
+                for j in range(2):
+                    at = slice(j * T + i, j * T + i + CH)
+                    b_ref[k, 0, at], b_ref[k, 1, at] = split(parts[0][j] + parts[1][j])
+                    b_ref[k, 2, at], b_ref[k, 3, at] = split(parts[0][j] - parts[1][j])
+
+        def along_rows(k):
+            for n, name in enumerate(("even", "odd")):
+                bh, bl = b_ref[k, 2 * n], b_ref[k, 2 * n + 1]
+                z = mm(lanes(tab(name + "h"), tab(name + "h"), tab(name + "l")), rows(bh, bl, bh))
+                for j in range(2):
+                    at = j * T + n * R
+                    part = slice(j * T, (j + 1) * T)
+                    zh, zl = split(lanes(z[:R, part], z[R:, part]))
+                    z_ref[k, at : at + R], z_ref[k, N + at : N + at + R] = zh, zl
+
+        def along_lanes(k, total):
             wi = lanes(tab("wih")[:, :T], tab("wil")[:, :T])
-            e = mm(zh, wi)
-            f = mm(zl, wi)
-            e = (e[:, :T] + e[:, T:]) + (f[:, :T] + f[:, T:])
+            e = mm(z_ref[k], wi)
+            e = (e[:N, :T] + e[:N, T:]) + (e[N:, :T] + e[N:, T:])
             field_ref[k] = e
             square = e * e
             return total + (square[:T] + square[T:])
 
-        intensity = lax.fori_loop(0, K, forward, zero, unroll=True)
+        intensity = zero
+        for step in range(K + 2):
+            if 1 <= step <= K:
+                along_rows(step - 1)
+            if step < K:
+                spread(step)
+            if step >= 2:
+                intensity = along_lanes(step - 2, intensity)
         wanted = rows(target_ref[pl.ds(0, R, stride=2), :], target_ref[pl.ds(1, R, stride=2), :])
         resist = 1.0 / (1.0 + jnp.exp(-SLOPE * (intensity - LEVEL)))
         miss = resist - wanted
@@ -366,33 +412,39 @@
 
         gr_ref[...] = jnp.zeros_like(gr_ref)
         gi_ref[...] = jnp.zeros_like(gi_ref)
-        weight2 = rows(weight, weight)
-
-        def adjoint(k, carry):
-            vh, vl = split(weight2 * field_ref[k])
-            v = lanes(vh, vl)
+        def weigh(k):
+            for j in range(2):
+                for i in range(0, T, CH):
+                    at = slice(j * T + i, j * T + i + CH)
+                    v_ref[k, at, :T], v_ref[k, at, T:] = split(weight[i : i + CH] * field_ref[k, at])
+
+        def from_lanes(k):
             wh, wl = tab("wh")[:T], tab("wl")[:T]
-            y = mm(v, rows(wh, wh)) + mm(v, rows(wl, wl))
-            y_r = lanes(y[:T, :T], y[T:, :T])
-            y_i = lanes(y[:T, T:], y[T:, T:])
+            v = v_ref[k]
+            y = mm(lanes(v, v), rows(wh, wh, wl, wl))
+            for n in range(2):
+                for j in range(2):
+                    part = slice(j * T, (j + 1) * T)
+                    yh, yl = split(lanes(y[n * R : (n + 1) * R, part], y[T + n * R : T + (n + 1) * R, part]))
+                    at = j * R
+                    y_ref[k, n, at : at + R], y_ref[k, n, T + at : T + at + R] = yh, yl
+
+        def gather(k):
             out = []
             for n in range(2):
-                half = slice(n * R, (n + 1) * R)
-                yh, yl = split(rows(y_r[half], y_i[half]))
-                y2 = rows(yh, yl)
+                y2 = y_ref[k, n]
                 bh = tab("bothh")[:, n * T : (n + 1) * T]
                 bl = tab("bothl")[:, n * T : (n + 1) * T]
-                out.append(mm(lanes(bh, bh), y2) + mm(lanes(bl, bl), y2))
+                out.append(mm(lanes(bh, bh, bl, bl), rows(y2, y2)))
             even, odd = out
-            first = even + odd
-            second = even - odd
-            for n, s in enumerate((first, second)):
-                at = slice(n * T, (n + 1) * T)
-                s_r, s_i = s[:T], s[T:]
-                h_r, h_i = hr_ref[k, at], hi_ref[k, at]
-                gr_ref[at] += h_r * s_r - h_i * s_i
-                gi_ref[at] += h_r * s_i + h_i * s_r
-            return carry
+            for i in range(0, T, CH):
+                parts = [(x[i : i + CH], x[T + i : T + i + CH]) for x in (even, odd)]
+                for n, sign in enumerate((1, -1)):
+                    at = slice(n * T + i, n * T + i + CH)
+                    s_r, s_i = (e + o if sign > 0 else e - o for e, o in zip(*parts))
+                    h_r, h_i = hr_ref[k, at], hi_ref[k, at]
+                    gr_ref[at] += h_r * s_r - h_i * s_i
+                    gi_ref[at] += h_r * s_i + h_i * s_r
 
         last = t == ITERS - 1
         reducing = None
@@ -403,7 +455,13 @@
                 value = jnp.where(line == n, jnp.sum(goal_part[n], axis=0, keepdims=True), value)
             reducing = reduce_start(0, value)
             pending += reducing
-        lax.fori_loop(0, K, adjoint, 0, unroll=True)
+        for step in range(K + 2):
+            if 1 <= step <= K:
+                from_lanes(step - 1)
+            if step < K:
+                weigh(step)
+            if step >= 2:
+                gather(step - 2)
         g = lanes(gr_ref[:, :T] + gr_ref[:, T:], gi_ref[:, :T] + gi_ref[:, T:])
         gh, gl = split(g)
         q = mm(lanes(tab("dh"), tab("dh"), tab("dl")), rows(gh, gl, gh))
@@ -426,23 +484,25 @@
         )
         if last:
             next_ref[...] = updated
+            put(0, next_ref, next_hbm)
             total = reduce_end(1, reducing)
             scale = 1.0 / (size_r * size_c * T * T)
             for n in range(ITERS):
                 goal_ref[n] = jnp.sum(total[n : n + 1]) * scale
         else:
             last_ref[...] = updated
+            put(1, last_ref, last_hbm)
             point = extrapolate(t + 1, updated, previous)
             previous = updated
             sent = send_point(t + 1, point)
             pending += sent
     for copy in pending:
         copy.wait_send()
+    for copy in stored:
+        copy.wait()
 
 
 def shards(size_r, size_c, mask, mask_prev, target, kernels, restart):
-    vmem = pl.BlockSpec(memory_space=pltpu.VMEM)
-    smem = pl.BlockSpec(memory_space=pltpu.SMEM)
     anywhere = pl.BlockSpec(memory_space=pltpu.HBM)
     rows_by, cols_by = factors(size_r, size_c)
     widest = max(rows_by[1] * cols_by[1], rows_by[0] * cols_by[0] * rows_by[2])
@@ -453,9 +513,15 @@
             jax.ShapeDtypeStruct((T, T), F32),
             jax.ShapeDtypeStruct((ITERS,), F32),
         ),
-        in_specs=[vmem, vmem, vmem, smem, anywhere, anywhere],
-        out_specs=(vmem, vmem, smem),
+        in_specs=[anywhere] * 6,
+        out_specs=(anywhere, anywhere, pl.BlockSpec(memory_space=pltpu.SMEM)),
         scratch_shapes=[
+            pltpu.VMEM((T, T), F32),
+            pltpu.VMEM((T, T), F32),
+            pltpu.VMEM((T, T), F32),
+            pltpu.VMEM((T, T), F32),
+            pltpu.VMEM((T, T), F32),
+            pltpu.SMEM((1, 1, ITERS), jnp.int32),
             pltpu.VMEM((K, KS, 2, KS), F32),
             pltpu.VMEM(TABLE.shape, BF16),
             pltpu.VMEM((2, KP, N), F32),
@@ -466,6 +532,11 @@
             pltpu.VMEM((N, N), F32),
             pltpu.VMEM((ITERS, T, T), F32),
             pltpu.VMEM((ITERS, T, T), F32),
+            pltpu.VMEM((K, 4, N, N), BF16),
+            pltpu.VMEM((K, 2 * N, N), BF16),
+            pltpu.VMEM((K, N, N), BF16),
+            pltpu.VMEM((K, 2, N, N), BF16),
+            pltpu.VMEM((2, N, T), F32),
             pltpu.VMEM((2 * ITERS, T, T), F32),
             pltpu.VMEM((2 * ITERS, 2, R, T), F32),
             pltpu.VMEM((2 * ITERS, 2, 2, R // 2, T), F32),
@@ -474,7 +545,7 @@
             pltpu.VMEM((ITERS, 8, T), F32),
             pltpu.VMEM((2, widest, 8, T), F32),
             pltpu.VMEM((2, 8, T), F32),
-            pltpu.SemaphoreType.DMA((2,)),
+            pltpu.SemaphoreType.DMA((8,)),
             pltpu.SemaphoreType.DMA((2 * ITERS, 8)),
             pltpu.SemaphoreType.DMA((2 * ITERS, 8)),
             pltpu.SemaphoreType.DMA((2, widest)),
@@ -488,19 +559,28 @@
     return pl.pallas_call(
         store,
         out_shape=tuple(jax.ShapeDtypeStruct(x.shape, x.dtype) for x in results),
-        in_specs=[vmem, vmem, vmem],
-        out_specs=(anywhere, anywhere, anywhere),
-        scratch_shapes=[pltpu.SemaphoreType.DMA((3,))],
+        in_specs=[anywhere] * 3,
+        out_specs=(anywhere,) * 3,
+        scratch_shapes=[
+            pltpu.VMEM((T, T), F32),
+            pltpu.VMEM((T, T), F32),
+            pltpu.VMEM((ITERS,), F32),
+            pltpu.SemaphoreType.DMA((2, 3)),
+        ],
         name="store",
     )(*results)
 
 
-def store(a_ref, b_ref, c_ref, next_ref, last_ref, goal_ref, sems):
-    pairs = ((a_ref, next_ref), (b_ref, last_ref), (c_ref, goal_ref))
-    copies = [pltpu.make_async_copy(x, y, sems.at[n]) for n, (x, y) in enumerate(pairs)]
-    for copy in copies:
+def store(a_hbm, b_hbm, c_hbm, next_hbm, last_hbm, goal_hbm, a_ref, b_ref, c_ref, sems):
+    trips = ((a_hbm, a_ref, next_hbm), (b_hbm, b_ref, last_hbm), (c_hbm, c_ref, goal_hbm))
+    there = [pltpu.make_async_copy(x, y, sems.at[0, n]) for n, (x, y, _) in enumerate(trips)]
+    back = [pltpu.make_async_copy(y, z, sems.at[1, n]) for n, (_, y, z) in enumerate(trips)]
+    for copy in there:
         copy.start()
-    for copy in copies:
+    for first, second in zip(there, back):
+        first.wait()
+        second.start()
+    for copy in back:
         copy.wait()
 
 

time: 58.2 us -> 53.3 us (0.916)
  Pallas kernels: 57.3 us -> 52.4 us
    pallas_call x1, Pallas kernels: 55.7 us -> 50.8 us  [shards(): pl.pallas_call(functools.partial(kernel, size_r, size_c), out_shape=(jax....]
where the time goes in v4:
time: 53.3 us; the launch traced here: 53.2 us
  Pallas kernels  52.4 us (98%)
  between operations  0.8 us (2%)
    pallas_call x1, Pallas kernels, shards(): pl.pallas_call(functools.partial(kernel, size_r, size_c), out_shape=(jax....  50.8 us
    pallas_call x1, Pallas kernels, shards(): pl.pallas_call(store, out_shape=tuple((jax.ShapeDtypeStruct(x.shape, x.dt...  1.55 us

profile of v4, /device:TPU:1, one launch (start us, length us, event | category | flops | bytes accessed | tf_op | source)
XLA Modules:
  0.0 53.2 jit_solution(15006165199643879794)
XLA Ops:
  0.6 50.8 %fista.1 = (f32[128,128]{1,0:T(8,128)}, f32[128,128]{1,0:T(8,128)}, f32[2]{0:T(128)}) custom-call(f32[128,128]{1,0:T(8,128)} %mask_hbm.1, f32[128,128]{1,0:T(8,128)} %prev_hbm.1, f32[128,128]{1,0:T(8,128)} %target_hbm.1, s32[1,1,2]{2,1,0:T(1,128)} %bitcast.3, f32[8,129,2,129]{3,2,1,0:T(2,128)} %bitcast.2, bf16[4608,256]{1,0:T(8,128)(2,1)} %constant.2.clone.table_hbm), custom_call_target="tpu_custom_call" | custom-call | tf_op jit(solution)/shard_map/fista/pallas_call | solution.py:509
  51.5 1.6 %store.1 = (f32[128,128]{1,0:T(8,128)}, f32[128,128]{1,0:T(8,128)}, f32[2]{0:T(128)}) custom-call(f32[128,128]{1,0:T(8,128)} %get-tuple-element.6.a_hbm, f32[128,128]{1,0:T(8,128)} %get-tuple-element.7.b_hbm, f32[2]{0:T(128)} %get-tuple-element.8.c_hbm), custom_call_target="tpu_custom_call" | custom-call | tf_op jit(solution)/shard_map/store/pallas_call | solution.py:559

commit v5 on v4

--- a/solution.py
+++ b/solution.py
@@ -220,32 +220,40 @@
         point_ref[t] = point
         return point
 
-    def exchange(slot, sign, beyond, beside, corner):
-        side_out[slot, 0], side_out[slot, 1] = pack(beside)
-        for h in range(2):
-            corner_out[slot, h, 0], corner_out[slot, h, 1] = pack(corner[h * R : (h + 1) * R])
-        pieces = []
+    def start(slot, n, dr, dc, source, target):
+        copy = pltpu.make_async_remote_copy(
+            src_ref=source,
+            dst_ref=target,
+            send_sem=send_sem.at[slot, n],
+            recv_sem=recv_sem.at[slot, n],
+            device_id=near[dr, dc],
+            device_id_type=MESH,
+        )
+        copy.start()
+        return copy
+
+    def send_corners(slot, sign, block):
         ways = (-sign, sign)
         for h in range(2):
-            for p in range(2):
-                pieces.append((ways[h], ways[p], corner_out.at[slot, h, p], corner_ref.at[slot, h, p]))
-        for h in range(2):
-            half = pl.ds(h * R, R)
-            pieces.append((ways[h], 0, beyond.at[half], ud_ref.at[slot, half]))
-        for p in range(2):
-            pieces.append((0, ways[p], side_out.at[slot, p], side_ref.at[slot, p]))
+            corner_out[slot, h, 0], corner_out[slot, h, 1] = pack(block[h * R : (h + 1) * R])
         copies = []
-        for n, (dr, dc, source, target) in enumerate(pieces):
-            copy = pltpu.make_async_remote_copy(
-                src_ref=source,
-                dst_ref=target,
-                send_sem=send_sem.at[slot, n],
-                recv_sem=recv_sem.at[slot, n],
-                device_id=near[dr, dc],
-                device_id_type=MESH,
+        for h, p in ((1, 1), (0, 0), (1, 0), (0, 1)):
+            copies.append(
+                start(slot, 2 * h + p, ways[h], ways[p], corner_out.at[slot, h, p], corner_ref.at[slot, h, p])
             )
-            copy.start()
-            copies.append(copy)
+        return copies
+
+    def send_beyond(slot, sign, ref):
+        ways = (-sign, sign)
+        halves = [pl.ds(h * R, R) for h in range(2)]
+        return [start(slot, 4 + h, ways[h], 0, ref.at[halves[h]], ud_ref.at[slot, halves[h]]) for h in range(2)]
+
+    def send_beside(slot, sign, block):
+        ways = (-sign, sign)
+        copies = []
+        for p, part in enumerate(pack(block)):
+            side_out[slot, p] = part
+            copies.append(start(slot, 6 + p, 0, ways[p], side_out.at[slot, p], side_ref.at[slot, p]))
         return copies
 
     def pack(block):
@@ -258,16 +266,19 @@
         first = first_lanes[: low.shape[0]]
         return rows(jnp.where(first, low, pltpu.roll(high, R, 1)), jnp.where(first, pltpu.roll(low, R, 1), high))
 
-    def arrived(slot):
-        corner = rows(*(unpack(corner_ref[slot, h, 0], corner_ref[slot, h, 1]) for h in range(2)))
-        return ud_ref[slot], unpack(side_ref[slot, 0], side_ref[slot, 1]), corner
+    def arrived(slot, copies):
+        for copy in copies:
+            copy.wait_recv()
+        return ud_ref[slot], unpack(side_ref[slot, 0], side_ref[slot, 1])
+
+    def arrived_corners(slot, copies):
+        for copy in copies:
+            copy.wait_recv()
+        return rows(*(unpack(corner_ref[slot, h, 0], corner_ref[slot, h, 1]) for h in range(2)))
 
     def send_point(t, point):
-        return exchange(2 * t, 1, point_ref.at[t], point, point)
-
-    def send_gradient(t, g):
-        own_ref[t] = g[T:, :T]
-        return exchange(2 * t + 1, -1, own_ref.at[t], g[:T, T:], g[T:, T:])
+        near_by = send_corners(2 * t, 1, point)
+        return near_by, send_beyond(2 * t, 1, point_ref.at[t]) + send_beside(2 * t, 1, point)
 
     def reduce_start(phase, value):
         me, peers = groups[phase]
@@ -307,7 +318,7 @@
     point = extrapolate(0, mask_ref[...], prev_ref[...])
     pl.semaphore_wait(barrier, len(everyone))
     sent = send_point(0, point)
-    pending = list(sent)
+    pending = sent[0] + sent[1]
 
     padded_ref[...] = jnp.zeros_like(padded_ref)
     for copy in loads[3:]:
@@ -330,15 +341,19 @@
     previous = mask_ref[...]
     objective = []
     for t in range(ITERS):
-        for copy in sent:
-            copy.wait_recv()
         zero = jnp.zeros((T, T), F32)
         rows_live = jnp.where(upper, has_down.astype(F32), has_up.astype(F32))
         lanes_live = jnp.where(first_lanes, has_right.astype(F32), has_left.astype(F32))
-        below, beside, corner = arrived(2 * t)
+        below, beside = arrived(2 * t, sent[1])
         below = below * rows_live
         beside = beside * lanes_live
-        corner = corner * (rows_live * lanes_live)
+        corner = arrived_corners(2 * t, sent[0]) * (rows_live * lanes_live)
+        xh, xl = split(rows(lanes(point, beside), lanes(below, corner)))
+        a = mm(lanes(xh, xh, xl), rows(tab("wh"), tab("wl"), tab("wh")))
+        ah, al = split(a)
+        q = mm(lanes(tab("dh"), tab("dh"), tab("dl")), rows(ah, al, ah))
+        m_ref[0] = q[:N, :T] + q[N:, T:]
+        m_ref[1] = q[:N, T:] - q[N:, :T]
         x = rows(lanes(point, beside), lanes(below, corner))
 
         strip = rows(x[N - 8 :], x[: T + 8])
@@ -355,14 +370,6 @@
         from_left = jnp.where((lane_id == 0) & (c == 0), zero, from_left)
         grad_tv = from_up + from_left - (flow_down + flow_side)[8 : T + 8, :T]
         length = (squared * inverse)[8 : T + 8, :T]
-
-        xh, xl = split(x)
-        a = mm(lanes(xh, xh, xl), rows(tab("wh"), tab("wl"), tab("wh")))
-        ah, al = split(a)
-        q = mm(lanes(tab("dh"), tab("dh"), tab("dl")), rows(ah, al, ah))
-        mr = q[:N, :T] + q[N:, T:]
-        mi = q[:N, T:] - q[N:, :T]
-        m_ref[0], m_ref[1] = mr, mi
 
         def spread(k):
             for i in range(0, T, CH):
@@ -449,10 +456,9 @@
         last = t == ITERS - 1
         reducing = None
         if last:
-            line = lax.broadcasted_iota(jnp.int32, (8, T), 0)
-            value = jnp.zeros((8, T), F32)
-            for n in range(ITERS):
-                value = jnp.where(line == n, jnp.sum(goal_part[n], axis=0, keepdims=True), value)
+            parts = [jnp.sum(goal_part[n], axis=0, keepdims=True) for n in range(ITERS)]
+            parts = [part + pltpu.roll(part, R, 1) for part in parts]
+            value = jnp.where(first_lanes[:1], parts[0], parts[1])
             reducing = reduce_start(0, value)
             pending += reducing
         for step in range(K + 2):
@@ -464,21 +470,30 @@
                 gather(step - 2)
         g = lanes(gr_ref[:, :T] + gr_ref[:, T:], gi_ref[:, :T] + gi_ref[:, T:])
         gh, gl = split(g)
-        q = mm(lanes(tab("dh"), tab("dh"), tab("dl")), rows(gh, gl, gh))
-        z = lanes(q[:N, :T] - q[N:, T:], q[:N, T:] + q[N:, :T])
-        zh, zl = split(z)
-        g = mm(lanes(zh, zh, zl), rows(tab("wih"), tab("wil"), tab("wih")))
-        sent = send_gradient(t, g)
-        pending += sent
+
+        def back(at):
+            dh, dl = (rows(tab(name)[at : at + T], tab(name)[N + at : N + at + T]) for name in ("dh", "dl"))
+            q = mm(lanes(dh, dh, dl), rows(gh, gl, gh))
+            zh, zl = split(lanes(q[:T, :T] - q[T:, T:], q[:T, T:] + q[T:, :T]))
+            return mm(lanes(zh, zh, zl), rows(tab("wih"), tab("wil"), tab("wih")))
+
+        slot = 2 * t + 1
+        halo = back(T)
+        sent_corners = send_corners(slot, -1, halo[:, T:])
+        own_ref[t] = halo[:, :T]
+        sent = send_beyond(slot, -1, own_ref.at[t])
+        g = back(0)
+        sent += send_beside(slot, -1, g[:, T:])
+        pending += sent_corners + sent
         if last:
             reducing = reduce_start(1, reduce_end(0, reducing))
             pending += reducing
-        for copy in sent:
-            copy.wait_recv()
         rows_live = jnp.where(upper, has_up.astype(F32), has_down.astype(F32))
         lanes_live = jnp.where(first_lanes, has_left.astype(F32), has_right.astype(F32))
-        below, beside, corner = arrived(2 * t + 1)
-        grad_data = 2.0 * (g[:T, :T] + below * rows_live + (beside + corner * rows_live) * lanes_live)
+        below, beside = arrived(slot, sent)
+        grad_data = g[:, :T] + below * rows_live + beside * lanes_live
+        corner = arrived_corners(slot, sent_corners)
+        grad_data = 2.0 * (grad_data + corner * (rows_live * lanes_live))
         updated = jnp.clip(
             point - STEP_SIZE * (grad_data + TV_WEIGHT * grad_tv) - STEP_SIZE * L1_WEIGHT, 0.0, 1.0
         )
@@ -488,14 +503,14 @@
             total = reduce_end(1, reducing)
             scale = 1.0 / (size_r * size_c * T * T)
             for n in range(ITERS):
-                goal_ref[n] = jnp.sum(total[n : n + 1]) * scale
+                goal_ref[n] = jnp.sum(jnp.where((lane_id[:1] < R) == (n == 0), total, 0.0)) * scale
         else:
             last_ref[...] = updated
             put(1, last_ref, last_hbm)
             point = extrapolate(t + 1, updated, previous)
             previous = updated
             sent = send_point(t + 1, point)
-            pending += sent
+            pending += sent[0] + sent[1]
     for copy in pending:
         copy.wait_send()
     for copy in stored:
@@ -543,8 +558,8 @@
             pltpu.VMEM((2 * ITERS, 2, R, T), F32),
             pltpu.VMEM((2 * ITERS, 2, 2, R // 2, T), F32),
             pltpu.VMEM((ITERS, 8, T), F32),
-            pltpu.VMEM((2, widest, 8, T), F32),
-            pltpu.VMEM((2, 8, T), F32),
+            pltpu.VMEM((2, widest, 1, T), F32),
+            pltpu.VMEM((2, 1, T), F32),
             pltpu.SemaphoreType.DMA((8,)),
             pltpu.SemaphoreType.DMA((2 * ITERS, 8)),
             pltpu.SemaphoreType.DMA((2 * ITERS, 8)),

time: 53.3 us -> 52.4 us (0.983)
  Pallas kernels: 52.4 us -> 51.4 us
    pallas_call x1, Pallas kernels: 50.8 us -> 49.9 us  [shards(): pl.pallas_call(functools.partial(kernel, size_r, size_c), out_shape=(jax....]
where the time goes in v5:
time: 52.4 us; the launch traced here: 52.2 us
  Pallas kernels  51.4 us (98%)
  between operations  0.8 us (2%)
    pallas_call x1, Pallas kernels, shards(): pl.pallas_call(functools.partial(kernel, size_r, size_c), out_shape=(jax....  49.9 us
    pallas_call x1, Pallas kernels, shards(): pl.pallas_call(store, out_shape=tuple((jax.ShapeDtypeStruct(x.shape, x.dt...  1.55 us

profile of v5, /device:TPU:1, one launch (start us, length us, event | category | flops | bytes accessed | tf_op | source)
XLA Modules:
  0.0 52.2 jit_solution(8463656508385429918)
XLA Ops:
  0.6 49.9 %fista.1 = (f32[128,128]{1,0:T(8,128)}, f32[128,128]{1,0:T(8,128)}, f32[2]{0:T(128)}) custom-call(f32[128,128]{1,0:T(8,128)} %mask_hbm.1, f32[128,128]{1,0:T(8,128)} %prev_hbm.1, f32[128,128]{1,0:T(8,128)} %target_hbm.1, s32[1,1,2]{2,1,0:T(1,128)} %bitcast.3, f32[8,129,2,129]{3,2,1,0:T(2,128)} %bitcast.2, bf16[4608,256]{1,0:T(8,128)(2,1)} %constant.2.clone.table_hbm), custom_call_target="tpu_custom_call" | custom-call | tf_op jit(solution)/shard_map/fista/pallas_call | solution.py:524
  50.5 1.6 %store.1 = (f32[128,128]{1,0:T(8,128)}, f32[128,128]{1,0:T(8,128)}, f32[2]{0:T(128)}) custom-call(f32[128,128]{1,0:T(8,128)} %get-tuple-element.6.a_hbm, f32[128,128]{1,0:T(8,128)} %get-tuple-element.7.b_hbm, f32[2]{0:T(128)} %get-tuple-element.8.c_hbm), custom_call_target="tpu_custom_call" | custom-call | tf_op jit(solution)/shard_map/store/pallas_call | solution.py:574

commit v6 on v5

--- a/solution.py
+++ b/solution.py
@@ -179,6 +179,8 @@
                         )
                     )
     groups.append(((z_high * cols_by[0] + z_low) * rows_by[2] + core, peers))
+
+    groups.reverse()
 
     def tab(name):
         first, end = PLACE[name]

time: 52.4 us -> 52 us (level)
  no operation moved by 1% of the time
where the time goes in v6:
time: 52 us; the launch traced here: 51.7 us
  Pallas kernels  50.9 us (98%)
  between operations  0.8 us (2%)
    pallas_call x1, Pallas kernels, shards(): pl.pallas_call(functools.partial(kernel, size_r, size_c), out_shape=(jax....  49.4 us
    pallas_call x1, Pallas kernels, shards(): pl.pallas_call(store, out_shape=tuple((jax.ShapeDtypeStruct(x.shape, x.dt...  1.55 us

profile of v6, /device:TPU:1, one launch (start us, length us, event | category | flops | bytes accessed | tf_op | source)
XLA Modules:
  0.0 51.7 jit_solution(4253093247969743726)
XLA Ops:
  0.6 49.4 %fista.1 = (f32[128,128]{1,0:T(8,128)}, f32[128,128]{1,0:T(8,128)}, f32[2]{0:T(128)}) custom-call(f32[128,128]{1,0:T(8,128)} %mask_hbm.1, f32[128,128]{1,0:T(8,128)} %prev_hbm.1, f32[128,128]{1,0:T(8,128)} %target_hbm.1, s32[1,1,2]{2,1,0:T(1,128)} %bitcast.3, f32[8,129,2,129]{3,2,1,0:T(2,128)} %bitcast.2, bf16[4608,256]{1,0:T(8,128)(2,1)} %constant.2.clone.table_hbm), custom_call_target="tpu_custom_call" | custom-call | tf_op jit(solution)/shard_map/fista/pallas_call | solution.py:526
  50.0 1.6 %store.1 = (f32[128,128]{1,0:T(8,128)}, f32[128,128]{1,0:T(8,128)}, f32[2]{0:T(128)}) custom-call(f32[128,128]{1,0:T(8,128)} %get-tuple-element.6.a_hbm, f32[128,128]{1,0:T(8,128)} %get-tuple-element.7.b_hbm, f32[2]{0:T(128)} %get-tuple-element.8.c_hbm), custom_call_target="tpu_custom_call" | custom-call | tf_op jit(solution)/shard_map/store/pallas_call | solution.py:576
